TPU v7x, 32 devices: a whole 2x2x4 slice. The times are simulated.
32 devices in a mesh: days: 2 (over x), tm: 8 (over z, y), sta: 2 (over core).
Axes of the slice: x: 2, y: 2, z: 4, core: 2. Of those that a mesh axis runs over, the one named last changes fastest.
Arguments:
- records: bfloat16 [2048, 2048], P('sta', ('days', 'tm')), parts along dimension 1, may hold values from -6 to 6
- following: bfloat16 [2048, 510], P('sta', 'days'), parts along dimension 1, may hold values from -6 to 6
- library: bfloat16 [32, 2048, 256], P(None, ('sta', 'tm')), may hold values from -6 to 6
- template_ids: int32 [2, 8], replicated, may hold values from 0 to 31
- channel_mask: int32 [32, 2048], replicated, may hold values 0 or 1
- station_group: int32 [2048], replicated, may hold values from 0 to 127
Outputs:
- detection: float32 [2, 8, 2048], P('sta', None, ('days', 'tm')), parts along dimension 2
There are 2 independent parts, one for each index of `days`. A program takes and returns all parts, laid end to end along the dimension named above; an argument that names none is the same for every part. Nothing has to cross between parts.
All inputs are finite; a program needn't handle non-finite values.
Results may differ from a plain program's by a relative error of at most 0.0003.
Values may be sent and summed in bfloat16 or wider, within the bound.
No kernel may reach another device: no remote copies, remote signals or barrier semaphores. Data moves between devices by JAX's collectives and lax.ppermute only.
A program may use at most 128 MiB of HBM per device.

v0:
```python
import jax
import jax.numpy as jnp
from jax import lax
from jax.sharding import PartitionSpec as P

W = 256
NB = 2
KB = 8
G = 128


epsilon = 1e-06


def inverse_norm(stream_rows, out_len):
    squares = jnp.square(stream_rows.astype(jnp.float32))
    running = jnp.cumsum(squares, axis=1)
    running = jnp.concatenate([jnp.zeros((running.shape[0], 1), jnp.float32), running], axis=1)
    energy = (running[:, W : W + out_len] - running[:, :out_len]) / W
    return 1.0 / jnp.sqrt(energy + epsilon)


def correlate(rows, temp_rows, out_len):
    block_size = rows.shape[0]
    slot_count = temp_rows.shape[0]
    kernel = jnp.transpose(temp_rows, (1, 0, 2)).reshape(block_size * slot_count, 1, W)
    result = lax.conv_general_dilated(
        rows[None],
        kernel,
        (1,),
        "VALID",
        dimension_numbers=("NCH", "OIH", "NCH"),
        feature_group_count=block_size,
        preferred_element_type=jnp.float32,
    )
    return result[0, :, :out_len].reshape(block_size, slot_count, out_len)


def station_terms(stream_rows, temps, weights, inverse):
    station_count = stream_rows.shape[0]
    out_len = inverse.shape[1]
    slot_count = temps.shape[0]
    size_limit = max(1, (1 << 22) // (W * out_len))
    block_size = max(
        (
            divisor
            for divisor in range(1, station_count + 1)
            if station_count % divisor == 0 and divisor <= size_limit
        )
    )
    turn_count = station_count // block_size
    rows_blocks = stream_rows.reshape(turn_count, block_size, stream_rows.shape[1])
    temp_blocks = jnp.moveaxis(temps.reshape(slot_count, turn_count, block_size, W), 1, 0)
    weight_blocks = jnp.moveaxis(weights.reshape(slot_count, turn_count, block_size), 1, 0)
    scale_blocks = inverse.reshape(turn_count, block_size, out_len)

    def advance(running, inputs):
        rows, temp_rows, weight, scale = inputs
        corr = correlate(rows, temp_rows, out_len)
        factor = jnp.transpose(weight)[:, :, None] * scale[:, None, :]
        return (running + jnp.sum(corr * factor, axis=0), None)

    start_zero = jnp.zeros((slot_count, out_len), jnp.float32)
    return lax.scan(advance, start_zero, (rows_blocks, temp_blocks, weight_blocks, scale_blocks))[0]


def shards(records, following, library, template_ids, channel_mask, station_group):
    sta_rows = records.shape[0]
    block_len = records.shape[1]
    sub_rows = library.shape[1]
    base = lax.axis_index("sta") * sta_rows
    onehot = (station_group[:, None] == jnp.arange(G, dtype=jnp.int32)[None, :]).astype(jnp.int32)
    counts = jnp.dot(channel_mask, onehot, preferred_element_type=jnp.int32)
    my_mask = lax.dynamic_slice_in_dim(channel_mask, base, sta_rows, 1)
    my_group = lax.dynamic_slice_in_dim(station_group, base, sta_rows, 0)
    per_station = jnp.take(counts, my_group, axis=1)
    scaled = my_mask.astype(jnp.float32) / jnp.sqrt(
        jnp.float32(W * G) * jnp.maximum(per_station, 1).astype(jnp.float32)
    )
    flat_ids = template_ids.reshape(-1)
    position = lax.axis_index("tm")
    moved = lax.all_to_all(records, "tm", split_axis=0, concat_axis=1, tiled=True)
    offset = position * sub_rows
    tail_rows = lax.dynamic_slice_in_dim(following, offset, sub_rows, 0)
    stream = jnp.concatenate([moved, tail_rows], axis=1)
    inverse = inverse_norm(stream, moved.shape[1])
    tmean = jnp.mean(jnp.square(library.astype(jnp.float32)), axis=2)
    factor = lax.dynamic_slice_in_dim(scaled, offset, sub_rows, 1) / jnp.sqrt(tmean + epsilon)
    chosen = jnp.take(library, flat_ids, axis=0)
    weights = jnp.take(factor, flat_ids, axis=0)
    partial_sum = station_terms(stream, chosen, weights, inverse)
    totals = lax.psum_scatter(partial_sum, "tm", scatter_dimension=1, tiled=True)
    return lax.psum_scatter(
        totals.reshape(NB, KB, block_len), "sta", scatter_dimension=0, tiled=True
    )


def solution(mesh):
    placed = (
        P("sta", ("days", "tm")),
        P("sta", "days"),
        P(None, ("sta", "tm"), None),
        P(),
        P(),
        P(),
    )
    return jax.shard_map(
        shards,
        mesh=mesh,
        in_specs=placed,
        out_specs=P("sta", None, ("days", "tm")),
        check_vma=False,
    )
```

profile of v0, /device:TPU:0, one launch (start us, length us, event | category | flops | bytes accessed | tf_op | source)
XLA Modules:
  0.0 271.5 jit_solution(17316995010624979843)
XLA Ops:
  6.5 7.5 %all-to-all-start = ((bf16[8,128,128]{2,1,0:T(8,128)(2,1)}), bf16[8,128,128]{2,1,0:T(8,128)(2,1)S(1)}, u32[]{:S(2)}, u32[]{:S(2)}) async-start(bf16[8,128,128]{2,1,0:T(8,128)(2,1)} %bitcast.60), calls=%async_computation | async-start | bytes 524288 | tf_op jit(solution)/shard_map/all_to_all | solution.py:82
  15.5 0.8 reshape.93
  16.3 0.8 reshape.92
  17.1 0.7 copy.50
  17.8 1.6 convolution_bitcast_fusion
  19.5 2.8 %gather_fusion.1 = s32[1024,32]{1,0:T(8,128)S(1)} fusion(s32[32,128]{0,1:T(8,128)S(1)} %copy.46, s32[1024]{0:T(1024)S(1)} %fusion.14), kind=kCustom, calls=%fused_computation.1 | custom fusion | bytes 266240 | tf_op jit(solution)/shard_map/jit(_take)/gather | solution.py:76
  22.3 0.8 copy.47
  23.8 1.6 gather_fusion
  25.5 0.7 fusion.13
  26.9 2.4 select_bitcast_fusion
  31.2 0.8 pad_maximum_fusion
  32.0 173.0 %while.11 = (s32[]{:T(128)}, f32[16,1024]{1,0:T(8,128)S(1)}, bf16[8,16,1279]{2,1,0:T(8,128)(2,1)}, bf16[8,16,16,256]{3,2,0,1:T(8,128)(2,1)}, f32[8,16,16]{1,2,0:...) while((s32[]{:T(128)}, f32[16,1024]{1,0:T(8,128)S(1)}, ...), condition=%wide.region_5.6_spmd.clone, body=%wide.region_3.5_spmd.clone.sunk | while | flops 2150383616 | bytes 5779415 | solution.py:64
  32.0 0.8 constant_dynamic-slice_fusion.6
  32.7 0.7 copy.65
  33.5 0.9 constant_dynamic-slice_fusion.7
  34.5 17.5 %fusion.23 = f32[1,256,1024]{1,0,2:T(1,128)S(1)} fusion(bf16[1,16,1279]{1,0,2:T(2,128)(2,1)S(1)} %copy.65, s32[256]{0:T(256)S(1)} %get-tuple-element.151, bf16[256,256]{0,1:T(8,128)(2,1)S(1)} %copy.67), kind=kOutput, calls=%fused_computation.5.clone.1 | convolution fusion | flops 2149580800 | bytes 1221600 | tf_op jit(solution)/shard_map/while/body/eval_jaxpr/conv_general_dilated | solution.py:27
  52.0 1.3 copy.68
  53.6 0.8 constant_dynamic-slice_fusion.6
  55.1 0.9 constant_dynamic-slice_fusion.7
  56.2 17.5 %fusion.23 = f32[1,256,1024]{1,0,2:T(1,128)S(1)} fusion(bf16[1,16,1279]{1,0,2:T(2,128)(2,1)S(1)} %copy.65, s32[256]{0:T(256)S(1)} %get-tuple-element.151, bf16[256,256]{0,1:T(8,128)(2,1)S(1)} %copy.67), kind=kOutput, calls=%fused_computation.5.clone.1 | convolution fusion | flops 2149580800 | bytes 1221600 | tf_op jit(solution)/shard_map/while/body/eval_jaxpr/conv_general_dilated | solution.py:27
  73.6 1.3 copy.68
  75.2 0.8 constant_dynamic-slice_fusion.6
  76.7 0.9 constant_dynamic-slice_fusion.7
  77.8 17.5 %fusion.23 = f32[1,256,1024]{1,0,2:T(1,128)S(1)} fusion(bf16[1,16,1279]{1,0,2:T(2,128)(2,1)S(1)} %copy.65, s32[256]{0:T(256)S(1)} %get-tuple-element.151, bf16[256,256]{0,1:T(8,128)(2,1)S(1)} %copy.67), kind=kOutput, calls=%fused_computation.5.clone.1 | convolution fusion | flops 2149580800 | bytes 1221600 | tf_op jit(solution)/shard_map/while/body/eval_jaxpr/conv_general_dilated | solution.py:27
  95.2 1.3 copy.68
  96.8 0.8 constant_dynamic-slice_fusion.6
  98.3 0.9 constant_dynamic-slice_fusion.7
  99.4 17.5 %fusion.23 = f32[1,256,1024]{1,0,2:T(1,128)S(1)} fusion(bf16[1,16,1279]{1,0,2:T(2,128)(2,1)S(1)} %copy.65, s32[256]{0:T(256)S(1)} %get-tuple-element.151, bf16[256,256]{0,1:T(8,128)(2,1)S(1)} %copy.67), kind=kOutput, calls=%fused_computation.5.clone.1 | convolution fusion | flops 2149580800 | bytes 1221600 | tf_op jit(solution)/shard_map/while/body/eval_jaxpr/conv_general_dilated | solution.py:27
  116.9 1.3 copy.68
  118.5 0.8 constant_dynamic-slice_fusion.6
  119.9 0.9 constant_dynamic-slice_fusion.7
  121.0 17.5 %fusion.23 = f32[1,256,1024]{1,0,2:T(1,128)S(1)} fusion(bf16[1,16,1279]{1,0,2:T(2,128)(2,1)S(1)} %copy.65, s32[256]{0:T(256)S(1)} %get-tuple-element.151, bf16[256,256]{0,1:T(8,128)(2,1)S(1)} %copy.67), kind=kOutput, calls=%fused_computation.5.clone.1 | convolution fusion | flops 2149580800 | bytes 1221600 | tf_op jit(solution)/shard_map/while/body/eval_jaxpr/conv_general_dilated | solution.py:27
  138.5 1.3 copy.68
  140.1 0.8 constant_dynamic-slice_fusion.6
  141.6 0.9 constant_dynamic-slice_fusion.7
  142.7 17.5 %fusion.23 = f32[1,256,1024]{1,0,2:T(1,128)S(1)} fusion(bf16[1,16,1279]{1,0,2:T(2,128)(2,1)S(1)} %copy.65, s32[256]{0:T(256)S(1)} %get-tuple-element.151, bf16[256,256]{0,1:T(8,128)(2,1)S(1)} %copy.67), kind=kOutput, calls=%fused_computation.5.clone.1 | convolution fusion | flops 2149580800 | bytes 1221600 | tf_op jit(solution)/shard_map/while/body/eval_jaxpr/conv_general_dilated | solution.py:27
  160.1 1.3 copy.68
  161.7 0.8 constant_dynamic-slice_fusion.6
  163.2 0.9 constant_dynamic-slice_fusion.7
  164.3 17.5 %fusion.23 = f32[1,256,1024]{1,0,2:T(1,128)S(1)} fusion(bf16[1,16,1279]{1,0,2:T(2,128)(2,1)S(1)} %copy.65, s32[256]{0:T(256)S(1)} %get-tuple-element.151, bf16[256,256]{0,1:T(8,128)(2,1)S(1)} %copy.67), kind=kOutput, calls=%fused_computation.5.clone.1 | convolution fusion | flops 2149580800 | bytes 1221600 | tf_op jit(solution)/shard_map/while/body/eval_jaxpr/conv_general_dilated | solution.py:27
  181.7 1.3 copy.68
  183.3 0.8 constant_dynamic-slice_fusion.6
  184.8 0.9 constant_dynamic-slice_fusion.7
  185.9 17.5 %fusion.23 = f32[1,256,1024]{1,0,2:T(1,128)S(1)} fusion(bf16[1,16,1279]{1,0,2:T(2,128)(2,1)S(1)} %copy.65, s32[256]{0:T(256)S(1)} %get-tuple-element.151, bf16[256,256]{0,1:T(8,128)(2,1)S(1)} %copy.67), kind=kOutput, calls=%fused_computation.5.clone.1 | convolution fusion | flops 2149580800 | bytes 1221600 | tf_op jit(solution)/shard_map/while/body/eval_jaxpr/conv_general_dilated | solution.py:27
  203.4 1.3 copy.68
  206.2 54.6 %reduce-scatter.2.cloned.1.call-done = f32[16,128]{1,0:T(8,128)} async-done(((f32[16,1024]{1,0:T(8,128)}), f32[16,128]{1,0:T(8,128)}) %reduce-scatter.2.cloned.1.call-update) | async-done | bytes 8208 | tf_op jit(solution)/shard_map/reduce_scatter | solution.py:92
  260.8 2.6 all-reduce.2
  263.4 1.2 constant_dynamic-slice_fusion.3
  (102 shorter events, 13.6 us)
Async XLA Ops:
  6.5 10.5 %copy-start = (bf16[1024,255]{1,0:T(8,128)(2,1)S(1)}, bf16[1024,255]{1,0:T(8,128)(2,1)}, u32[]{:S(2)}) copy-start(bf16[1024,255]{1,0:T(8,128)(2,1)} %param.9) | copy-start | bytes 1566724
  6.5 16.6 %copy-start.1 = (bf16[32,128,256]{2,1,0:T(8,128)(2,1)S(1)}, bf16[32,128,256]{2,1,0:T(8,128)(2,1)}, u32[]{:S(2)}) copy-start(bf16[32,128,256]{2,1,0:T(8,128)(2,1)} %param.10) | copy-start | bytes 6291460
  6.5 22.8 %all-to-all-start = ((bf16[8,128,128]{2,1,0:T(8,128)(2,1)}), bf16[8,128,128]{2,1,0:T(8,128)(2,1)S(1)}, u32[]{:S(2)}, u32[]{:S(2)}) async-start(bf16[8,128,128]{2,1,0:T(8,128)(2,1)} %bitcast.60), calls=%async_computation | async-start | bytes 524288 | tf_op jit(solution)/shard_map/all_to_all | solution.py:82
  14.1 246.7 %reduce-scatter.2.cloned.1.call-start = ((), (), s32[]{:S(2)}) async-start(), calls=%async_computation.2 | async-start | bytes 73728 | tf_op jit(solution)/shard_map/reduce_scatter | solution.py:92
  17.1 0.7 copy-start.3
  23.2 2.3 copy-start.5
  25.5 4.2 %copy-start.6 = (bf16[128,255]{0,1:T(8,128)(2,1)S(1)}, bf16[128,255]{0,1:T(8,128)(2,1)}, u32[]{:S(2)}) copy-start(bf16[128,255]{0,1:T(8,128)(2,1)} %copy.50) | copy-start | bytes 195844
  30.3 0.8 copy-start.4
  30.6 1.4 copy-start.8
  32.0 173.6 %copy-start.7 = (u32[32]{0:T(128)S(1)}, u32[32]{0:T(128)}, u32[]{:S(2)}) copy-start(u32[32]{0:T(128)} %constant.105) | copy-start | bytes 388
  204.9 0.6 copy-start.2
Sparse Core Ops, SparseCore 0:
  205.7 55.0 reduce-scatter.1
where the time goes:
time: 273 us; the launch traced here: 271 us
  matrix products  141 us (52%)
  waiting for transfers between devices  54.6 us (20%)
  local copies, waits for them, and re-layouts  42.9 us (16%)
  between operations  13.6 us (5%)
  other arithmetic  8.16 us (3%)
  starting transfers between devices  7.58 us (3%)
    conv_general_dilated x8, matrix products, correlate(): lax.conv_general_dilated(rows[None], kernel, (1,), 'VALID', dimension_num...  140 us
    reduce_scatter x1, waiting for transfers between devices, shards(): lax.psum_scatter(partial_sum, 'tm', scatter_dimension=1, tiled=True)  54.6 us
    dynamic_slice x32, local copies, waits for them, and re-layouts, station_terms(): lax.scan(advance, start_zero, (rows_blocks, temp_blocks, weight_blocks, s...  19.6 us
    conv_general_dilated x8, local copies, waits for them, and re-layouts, correlate(): lax.conv_general_dilated(rows[None], kernel, (1,), 'VALID', dimension_num...  10.6 us
    all_to_all x1, starting transfers between devices, shards(): lax.all_to_all(records, 'tm', split_axis=0, concat_axis=1, tiled=True)  7.54 us
  transfers between devices with their start and end apart: 2, of which 1 were waited for; matrix products, arithmetic and copies ran while one was open for 6% of the time, Pallas kernels for 0%

commit v1 on v0

v1 whole, which is shorter than its diff:
```python
import functools

import jax
import jax.numpy as jnp
from jax import lax
from jax.experimental import pallas as pl
from jax.experimental.pallas import tpu as pltpu
from jax.sharding import PartitionSpec as P

W = 256
NB = 2
KB = 8
G = 128
SLOTS = NB * KB
PH = 8
LANES = 128
TAPS = W // PH
VMEM = 56 << 20

epsilon = 1e-06


def lane_ids(shape):
    return lax.broadcasted_iota(jnp.int32, shape, len(shape) - 1)


def shifted(here, after, by):
    if by == 0:
        return here
    lane = lane_ids(here.shape)
    return pltpu.roll(jnp.where(lane < by, after, here), LANES - by, here.ndim - 1)


def prepare_kernel(chunk, ids, library, mask, group, shifts, coef, picked, wide, rows, made, in_sem, out_sem):
    stations = library.shape[1]
    total = mask.shape[1]
    for k in range(SLOTS):
        pltpu.make_async_copy(library.at[ids[k // KB, k % KB]], picked.at[k], in_sem).start()

    for k in range(SLOTS):
        rows[pl.ds(k, 1), :] = mask[pl.ds(ids[k // KB, k % KB], 1), :].astype(jnp.float32)
    members = lax.broadcasted_iota(jnp.int32, (G, total), 0) == group[...]
    counts = lax.dot_general(
        rows[...].astype(jnp.bfloat16),
        members.astype(jnp.float32).astype(jnp.bfloat16),
        (((1,), (1,)), ((), ())),
        preferred_element_type=jnp.float32,
    )
    first = lax.axis_index("sta") * (stations * lax.axis_size("tm")) + lax.axis_index("tm") * stations
    block = pl.multiple_of(first // LANES * LANES, LANES)
    own_group = jnp.broadcast_to(group[:, pl.ds(block, LANES)], (G, LANES))
    own_mask = rows[:, pl.ds(block, LANES)]
    own = (lax.broadcasted_iota(jnp.int32, (G, LANES), 0) == own_group).astype(jnp.float32)
    per_station = jnp.dot(counts, own, preferred_element_type=jnp.float32, precision=lax.Precision.HIGHEST)
    scaled = own_mask / jnp.sqrt(jnp.float32(W * G) * jnp.maximum(per_station, 1.0))
    if stations % LANES:
        scaled = pltpu.roll(scaled, LANES - (first - block), 1)
    scaled = jnp.concatenate([scaled, jnp.zeros((LANES - SLOTS, LANES), jnp.float32)], axis=0).T

    for k in range(SLOTS):
        pltpu.make_async_copy(library.at[0], picked.at[k], in_sem).wait()
    for k in range(SLOTS):
        values = picked[k].astype(jnp.float32)
        wide[k] = values
        tmean = jnp.sum(values * values, axis=1, keepdims=True) / W
        value = scaled[:stations, k : k + 1] / jnp.sqrt(tmean + epsilon)
        coef[pl.ds(k * stations, stations), :] = jnp.broadcast_to(value, (stations, LANES))

    lane = lane_ids((PH, LANES))
    row = lax.broadcasted_iota(jnp.int32, (PH, LANES), 0)
    inside = lane >= row

    def station(s):
        for pair in range(SLOTS // 2):
            halves = []
            for k in (2 * pair, 2 * pair + 1):
                template = wide[k, pl.ds(s, 1), :]
                turned = [
                    pltpu.roll(
                        jnp.broadcast_to(template[:, h * LANES : (h + 1) * LANES], (PH, LANES)), 0, 1, stride=1, stride_axis=0
                    )
                    for h in range(W // LANES)
                ]
                halves.append(
                    jnp.concatenate(
                        [jnp.where(inside, turned[h], turned[h - 1]) for h in range(W // LANES)], axis=1
                    )
                )
            made[s, 2 * PH * pair : 2 * PH * (pair + 1), :] = jnp.concatenate(halves, axis=0).astype(jnp.bfloat16)

    def part(c, carry):
        def step(i, inner):
            station(c * chunk + i)
            return inner

        lax.fori_loop(0, chunk, step, 0, unroll=4)
        span = pl.ds(c * chunk, chunk)
        pltpu.make_async_copy(made.at[span], shifts.at[span], out_sem).start()
        return carry

    lax.fori_loop(0, stations // chunk, part, 0)
    pltpu.make_async_copy(made, shifts, out_sem).wait()


def prepare(template_ids, library, channel_mask, station_group):
    stations = library.shape[1]
    total = channel_mask.shape[1]
    chunk = min(16, stations)
    return pl.pallas_call(
        functools.partial(prepare_kernel, chunk),
        out_shape=(
            jax.ShapeDtypeStruct((stations, SLOTS * PH, W), jnp.bfloat16),
            jax.ShapeDtypeStruct((SLOTS * stations, LANES), jnp.float32),
        ),
        in_specs=[
            pl.BlockSpec(memory_space=pltpu.SMEM),
            pl.BlockSpec(memory_space=pl.ANY),
            pl.BlockSpec(memory_space=pltpu.VMEM),
            pl.BlockSpec(memory_space=pltpu.VMEM),
        ],
        out_specs=(pl.BlockSpec(memory_space=pl.ANY), pl.BlockSpec(memory_space=pltpu.VMEM)),
        scratch_shapes=[
            pltpu.VMEM((SLOTS, stations, W), jnp.bfloat16),
            pltpu.VMEM((SLOTS, stations, W), jnp.float32),
            pltpu.VMEM((SLOTS, total), jnp.float32),
            pltpu.VMEM((stations, SLOTS * PH, W), jnp.bfloat16),
            pltpu.SemaphoreType.DMA,
            pltpu.SemaphoreType.DMA,
        ],
        compiler_params=pltpu.CompilerParams(vmem_limit_bytes=VMEM),
        cost_estimate=pl.CostEstimate(flops=10_000_000, bytes_accessed=20_000_000, transcendentals=0),
        name="prepare",
    )(template_ids, library, channel_mask, station_group.reshape(1, total))


def correlate_kernel(unroll, chunk, moved, following, shifts, coef, out, held, tail, phases, inverse, sums, sems, tail_sem):
    owners, stations, block_len = moved.shape
    width = block_len // PH
    tiles = owners * block_len // (LANES * PH)
    per_tile = LANES // width
    position = lax.axis_index("tm")

    tail_copy = pltpu.make_async_copy(following.at[pl.ds(position * stations, stations)], tail, tail_sem)
    tail_copy.start()
    loads = [
        pltpu.make_async_copy(shifts.at[pl.ds(c * chunk, chunk)], held.at[pl.ds(c * chunk, chunk)], sems.at[c])
        for c in range(stations // chunk)
    ]
    for load in loads:
        load.start()

    time = lax.broadcasted_iota(jnp.int32, (W, W), 0)
    place = lax.broadcasted_iota(jnp.int32, (W, W), 1)
    order = (time == place % TAPS * PH + place // TAPS).astype(jnp.float32).astype(jnp.bfloat16)
    lane = lane_ids((stations, LANES))
    pieces = LANES // TAPS
    each = W // block_len
    for j in range(tiles):
        split = [
            jnp.dot(
                jnp.concatenate([moved[(j * pieces + q) * each + e] for e in range(each)], axis=1),
                order,
                preferred_element_type=jnp.float32,
            )
            for q in range(pieces)
        ]
        for p in range(PH):
            half, at = p // pieces, p % pieces
            value = None
            for q in range(pieces):
                piece = split[q][:, half * LANES : (half + 1) * LANES]
                if q != at:
                    piece = pltpu.roll(piece, (TAPS * (q - at)) % LANES, 1)
                value = piece if value is None else jnp.where(lane >= TAPS * q, piece, value)
            phases[j, pl.ds(p * stations, stations), :] = value
    tail_copy.wait()
    last = jnp.concatenate([tail[...], jnp.zeros((stations, 1), jnp.bfloat16)], axis=1)
    split = jnp.dot(last, order, preferred_element_type=jnp.float32)
    for p in range(PH):
        half, at = p // pieces, p % pieces
        piece = split[:, half * LANES : (half + 1) * LANES]
        phases[tiles, pl.ds(p * stations, stations), :] = pltpu.roll(piece, (-TAPS * at) % LANES, 1) if at else piece

    def norms(g, carry):
        windows = []
        for p in range(PH):
            at = pl.ds(p * stations + g * 8, 8)
            values = [jnp.square(phases[j, at, :]) for j in range(tiles + 1)]
            by = 1
            while by < TAPS:
                values = [v + shifted(v, values[min(j + 1, tiles)], by) for j, v in enumerate(values)]
                by *= 2
            windows.append(values)
        for j in range(tiles):
            later = [None] * (PH + 1)
            for p in reversed(range(PH)):
                later[p] = windows[p][j] if later[p + 1] is None else windows[p][j] + later[p + 1]
            before = None
            for p in range(PH):
                energy = later[p] if before is None else later[p] + before
                inverse[j, pl.ds(p * stations + g * 8, 8), :] = lax.rsqrt(energy / W + epsilon)
                following_one = shifted(windows[p][j], windows[p][j + 1], 1)
                before = following_one if before is None else before + following_one
        return carry

    lax.fori_loop(0, stations // 8, norms, 0, unroll=2)

    row = lax.broadcasted_iota(jnp.int32, (SLOTS * PH, LANES), 0) % PH
    inside = lane_ids((SLOTS * PH, LANES)) >= row
    nothing = jnp.zeros((SLOTS * PH, LANES), jnp.bfloat16)

    def station(s, totals):
        templates = held[s]
        head = templates[:, :LANES]
        main = jnp.concatenate([jnp.where(inside, head, nothing), templates[:, LANES:]], axis=1)
        rest = jnp.where(inside, nothing, head)[:, : 2 * PH]
        gains = coef[pl.ds(s, SLOTS, stride=stations), :]
        own = [phases[j, pl.ds(s, PH, stride=stations), :] for j in range(tiles + 1)]
        results = []
        for j in range(tiles):
            window = [shifted(own[j], own[j + 1], by) for by in range(TAPS + 1)]
            window.append(jnp.zeros_like(own[j]))
            pairs = [
                jnp.concatenate(window[2 * i : 2 * i + 2], axis=0).astype(jnp.bfloat16) for i in range(TAPS // 2 + 1)
            ]
            corr = jnp.dot(main, jnp.concatenate(pairs[:-1], axis=0), preferred_element_type=jnp.float32)
            corr = corr + jnp.dot(rest, pairs[-1], preferred_element_type=jnp.float32)
            scale = inverse[j, pl.ds(s, PH, stride=stations), :]
            results.append(
                totals[j] + (corr.reshape(SLOTS, PH, LANES) * scale[None]) * gains[:, None, :]
            )
        return tuple(results)

    totals = tuple(jnp.zeros((SLOTS, PH, LANES), jnp.float32) for _ in range(tiles))
    for c, load in enumerate(loads):
        load.wait()
        totals = lax.fori_loop(c * chunk, (c + 1) * chunk, station, totals, unroll=unroll)

    lane = lane_ids((PH, LANES))
    for d in range(owners):
        j, at = d // per_tile, d % per_tile
        for b in range(NB):
            value = None
            for k in range(KB):
                piece = totals[j][b * KB + k]
                if k != at:
                    piece = pltpu.roll(piece, (width * (k - at)) % LANES, 1)
                value = piece if value is None else jnp.where(lane >= width * k, piece, value)
            out[d, b] = value


def correlate(moved, following, shifts, coef):
    owners, stations, block_len = moved.shape
    tiles = owners * block_len // (LANES * PH)
    chunk = min(32, stations)
    return pl.pallas_call(
        functools.partial(correlate_kernel, 16, chunk),
        out_shape=jax.ShapeDtypeStruct((owners, NB, PH, LANES), jnp.float32),
        in_specs=[
            pl.BlockSpec(memory_space=pltpu.VMEM),
            pl.BlockSpec(memory_space=pl.ANY),
            pl.BlockSpec(memory_space=pl.ANY),
            pl.BlockSpec(memory_space=pltpu.VMEM),
        ],
        out_specs=pl.BlockSpec(memory_space=pltpu.VMEM),
        scratch_shapes=[
            pltpu.VMEM(shifts.shape, jnp.bfloat16),
            pltpu.VMEM((stations, following.shape[1]), jnp.bfloat16),
            pltpu.VMEM((tiles + 1, PH * stations, LANES), jnp.float32),
            pltpu.VMEM((tiles, PH * stations, LANES), jnp.float32),
            pltpu.VMEM((8, LANES), jnp.float32),
            pltpu.SemaphoreType.DMA((stations // chunk,)),
            pltpu.SemaphoreType.DMA,
        ],
        compiler_params=pltpu.CompilerParams(vmem_limit_bytes=VMEM),
        cost_estimate=pl.CostEstimate(flops=1_200_000_000, bytes_accessed=10_000_000, transcendentals=0),
        name="correlate",
    )(moved, following, shifts, coef)


def finish_kernel(parts, out):
    total = jnp.sum(parts[...], axis=0)
    width = LANES // KB
    lane = lane_ids((KB, LANES))
    source = lax.broadcasted_iota(jnp.int32, (KB, LANES), 0) * width + lane // PH
    value = None
    for p in range(PH):
        spread = jnp.take_along_axis(jnp.broadcast_to(total[p : p + 1, :], (KB, LANES)), source, axis=1)
        value = spread if value is None else jnp.where(lane % PH == p, spread, value)
    out[0] = value


def finish(parts):
    return pl.pallas_call(
        finish_kernel,
        out_shape=jax.ShapeDtypeStruct((1, KB, LANES), jnp.float32),
        in_specs=[pl.BlockSpec(memory_space=pltpu.VMEM)],
        out_specs=pl.BlockSpec(memory_space=pltpu.VMEM),
        name="finish",
    )(parts)


def shards(records, following, library, template_ids, channel_mask, station_group):
    owners = lax.axis_size("tm")
    block_len = records.shape[1]
    stations = library.shape[1]
    moved = lax.all_to_all(records.reshape(owners, stations, block_len), "tm", split_axis=0, concat_axis=0)
    shifts, coef = prepare(template_ids, library, channel_mask, station_group)
    partial_sum = correlate(moved, following, shifts, coef)
    parts = lax.all_to_all(
        partial_sum.reshape(owners * NB, PH, LANES), ("tm", "sta"), split_axis=0, concat_axis=0
    )
    return finish(parts)


def solution(mesh):
    placed = (
        P("sta", ("days", "tm")),
        P("sta", "days"),
        P(None, ("sta", "tm"), None),
        P(),
        P(),
        P(),
    )
    return jax.shard_map(
        shards,
        mesh=mesh,
        in_specs=placed,
        out_specs=P("sta", None, ("days", "tm")),
        check_vma=False,
    )
```

time: 273 us -> 49.9 us (0.18)
  matrix products: 141 us -> 0 us
  waiting for transfers between devices: 54.6 us -> 0.01 us
  local copies, waits for them, and re-layouts: 42.9 us -> 0.68 us
  Pallas kernels: 0 us -> 28.4 us
  between operations: 13.6 us -> 0.03 us
  blocking collectives: 2.59 us -> 13.1 us
  other arithmetic: 8.16 us -> 0 us
    conv_general_dilated x8 -> x0, matrix products: 140 us -> none  [correlate(): lax.conv_general_dilated(rows[None], kernel, (1,), 'VALID', dimension_num...]
    reduce_scatter x1 -> x0, waiting for transfers between devices: 54.6 us -> none  [shards(): lax.psum_scatter(partial_sum, 'tm', scatter_dimension=1, tiled=True)]
    pallas_call x0 -> x3, Pallas kernels: none -> 28.4 us  [the longest x1 15.7 us: correlate(): pl.pallas_call(functools.partial(correlate_kernel, 16, chunk), out_shape=...]
    dynamic_slice x34 -> x0, local copies, waits for them, and re-layouts: 20.4 us -> none  [the longest x32 19.6 us: station_terms(): lax.scan(advance, start_zero, (rows_blocks, temp_blocks, weight_blocks, s...]
    all_to_all x0 -> x1, blocking collectives: none -> 13.1 us  [shards(): lax.all_to_all(partial_sum.reshape(owners * NB, PH, LANES), ('tm', 'sta')...]
    conv_general_dilated x8 -> x0, local copies, waits for them, and re-layouts: 10.6 us -> none  [correlate(): lax.conv_general_dilated(rows[None], kernel, (1,), 'VALID', dimension_num...]
    gather x5 -> x0, local copies, waits for them, and re-layouts: 5.94 us -> none  [the longest x2 3.63 us: shards(): per_station = jnp.take(counts, my_group, axis=1)]
  transfers between devices with their start and end apart: 2 -> 1, of which waited for: 1 -> 0; matrix products, arithmetic and copies ran while one was open for 6% -> 0% of each run, Pallas kernels for 0% -> 22%
where the time goes in v1:
time: 49.9 us; the launch traced here: 49.5 us
  Pallas kernels  28.4 us (57%)
  blocking collectives  13.1 us (26%)
  starting transfers between devices  7.28 us (15%)
  local copies, waits for them, and re-layouts  0.68 us (1%)
    pallas_call x1, Pallas kernels, correlate(): pl.pallas_call(functools.partial(correlate_kernel, 16, chunk), out_shape=...  15.7 us
    all_to_all x1, blocking collectives, shards(): lax.all_to_all(partial_sum.reshape(owners * NB, PH, LANES), ('tm', 'sta')...  13.1 us
    pallas_call x1, Pallas kernels, prepare(): pl.pallas_call(functools.partial(prepare_kernel, chunk), out_shape=(jax.S...  11.1 us
    all_to_all x1, starting transfers between devices, shards(): lax.all_to_all(records.reshape(owners, stations, block_len), 'tm', split_...  7.28 us
    pallas_call x1, Pallas kernels, finish(): pl.pallas_call(finish_kernel, out_shape=jax.ShapeDtypeStruct((1, KB, LANE...  1.52 us
  transfers between devices with their start and end apart: 1, of which 0 were waited for; matrix products, arithmetic and copies ran while one was open for 0% of the time, Pallas kernels for 22%

profile of v1, /device:TPU:0, one launch (start us, length us, event | category | flops | bytes accessed | tf_op | source)
XLA Modules:
  0.0 49.5 jit_solution(4830830119719478811)
XLA Ops:
  0.0 7.3 %all-to-all-start = ((bf16[8,128,128]{2,1,0:T(8,128)(2,1)}), bf16[8,128,128]{2,1,0:T(8,128)(2,1)S(1)}, u32[]{:S(2)}, u32[]{:S(2)}) async-start(bf16[8,128,128]{2,1,0:T(8,128)(2,1)} %bitcast.4), calls=%async_computation | async-start | bytes 524288 | tf_op jit(solution)/shard_map/all_to_all | solution.py:307
  7.3 11.1 %prepare.1 = (bf16[128,128,256]{2,1,0:T(8,128)(2,1)}, f32[2048,128]{1,0:T(8,128)}) custom-call(s32[2,8]{1,0:T(2,128)} %ids.1, bf16[32,128,256]{2,1,0:T(8,128)(2,1)} %library.1, s32[32,2048]{1,0:T(8,128)} %mask.1, s32[1,2048]{1,0:T(1,128)} %bitcast.5), custom_call_target="tpu_custom_call" | custom-call | flops 10000000 | bytes 20000000 | tf_op jit(solution)/shard_map/prepare/pallas_call | solution.py:109
  18.4 0.0 all-to-all-done.moved
  18.4 0.0 copy-start
  18.4 0.7 %copy-done = bf16[8,128,128]{2,1,0:T(8,128)(2,1)} copy-done((bf16[8,128,128]{2,1,0:T(8,128)(2,1)}, bf16[8,128,128]{2,1,0:T(8,128)(2,1)S(1)}, u32[]{:S(2)}) %copy-start) | copy-done | bytes 262168
  19.1 15.7 %correlate.1 = f32[8,2,8,128]{3,2,1,0:T(8,128)} custom-call(bf16[8,128,128]{2,1,0:T(8,128)(2,1)} %copy-done, bf16[1024,255]{1,0:T(8,128)(2,1)} %following.1, bf16[128,128,256]{2,1,0:T(8,128)(2,1)} %get-tuple-element.7.shifts, f32[2048,128]{1,0:T(8,128)} %get-tuple-element.8.coef), custom_call_target="tpu_custom_call" | custom-call | flops 1200000000 | bytes 10000000 | tf_op jit(solution)/shard_map/correlate/pallas_call | solution.py:256
  34.8 13.1 %all_to_all.10.parts = f32[16,8,128]{2,1,0:T(8,128)} all-to-all(f32[16,8,128]{2,1,0:T(8,128)} %bitcast.3), channel_id=1, replica_groups=mesh['days'=2,'tm'=8,'sta'=2] {'tm','sta'}, dimensions={0} | all-to-all | bytes 131072 | tf_op jit(solution)/shard_map/all_to_all | solution.py:310
  48.0 1.5 %finish.1 = f32[1,8,128]{2,1,0:T(8,128)} custom-call(f32[16,8,128]{2,1,0:T(8,128)} %all_to_all.10.parts), custom_call_target="tpu_custom_call" | custom-call | tf_op jit(solution)/shard_map/finish/pallas_call | solution.py:294
Async XLA Ops:
  0.0 18.4 %all-to-all-start = ((bf16[8,128,128]{2,1,0:T(8,128)(2,1)}), bf16[8,128,128]{2,1,0:T(8,128)(2,1)S(1)}, u32[]{:S(2)}, u32[]{:S(2)}) async-start(bf16[8,128,128]{2,1,0:T(8,128)(2,1)} %bitcast.4), calls=%async_computation | async-start | bytes 524288 | tf_op jit(solution)/shard_map/all_to_all | solution.py:307
  18.4 0.7 %copy-start = (bf16[8,128,128]{2,1,0:T(8,128)(2,1)}, bf16[8,128,128]{2,1,0:T(8,128)(2,1)S(1)}, u32[]{:S(2)}) copy-start(bf16[8,128,128]{2,1,0:T(8,128)(2,1)S(1)} %all-to-all-done.moved) | copy-start | bytes 786436

commit v2 on v1

--- a/solution.py
+++ b/solution.py
@@ -15,7 +15,7 @@
 PH = 8
 LANES = 128
 TAPS = W // PH
-VMEM = 56 << 20
+VMEM = 24 << 20
 
 epsilon = 1e-06
 
@@ -31,7 +31,7 @@
     return pltpu.roll(jnp.where(lane < by, after, here), LANES - by, here.ndim - 1)
 
 
-def prepare_kernel(chunk, ids, library, mask, group, shifts, coef, picked, wide, rows, made, in_sem, out_sem):
+def prepare_kernel(ids, library, mask, group, made, coef, picked, wide, rows, in_sem):
     stations = library.shape[1]
     total = mask.shape[1]
     for k in range(SLOTS):
@@ -88,29 +88,21 @@
                 )
             made[s, 2 * PH * pair : 2 * PH * (pair + 1), :] = jnp.concatenate(halves, axis=0).astype(jnp.bfloat16)
 
-    def part(c, carry):
-        def step(i, inner):
-            station(c * chunk + i)
-            return inner
-
-        lax.fori_loop(0, chunk, step, 0, unroll=4)
-        span = pl.ds(c * chunk, chunk)
-        pltpu.make_async_copy(made.at[span], shifts.at[span], out_sem).start()
+    def step(s, carry):
+        station(s)
         return carry
 
-    lax.fori_loop(0, stations // chunk, part, 0)
-    pltpu.make_async_copy(made, shifts, out_sem).wait()
+    lax.fori_loop(0, stations, step, 0, unroll=4)
 
 
 def prepare(template_ids, library, channel_mask, station_group):
     stations = library.shape[1]
     total = channel_mask.shape[1]
-    chunk = min(16, stations)
     return pl.pallas_call(
-        functools.partial(prepare_kernel, chunk),
+        prepare_kernel,
         out_shape=(
-            jax.ShapeDtypeStruct((stations, SLOTS * PH, W), jnp.bfloat16),
-            jax.ShapeDtypeStruct((SLOTS * stations, LANES), jnp.float32),
+            pltpu.VMEM((stations, SLOTS * PH, W), jnp.bfloat16),
+            pltpu.VMEM((SLOTS * stations, LANES), jnp.float32),
         ),
         in_specs=[
             pl.BlockSpec(memory_space=pltpu.SMEM),
@@ -118,13 +110,11 @@
             pl.BlockSpec(memory_space=pltpu.VMEM),
             pl.BlockSpec(memory_space=pltpu.VMEM),
         ],
-        out_specs=(pl.BlockSpec(memory_space=pl.ANY), pl.BlockSpec(memory_space=pltpu.VMEM)),
+        out_specs=(pl.BlockSpec(memory_space=pltpu.VMEM), pl.BlockSpec(memory_space=pltpu.VMEM)),
         scratch_shapes=[
             pltpu.VMEM((SLOTS, stations, W), jnp.bfloat16),
             pltpu.VMEM((SLOTS, stations, W), jnp.float32),
             pltpu.VMEM((SLOTS, total), jnp.float32),
-            pltpu.VMEM((stations, SLOTS * PH, W), jnp.bfloat16),
-            pltpu.SemaphoreType.DMA,
             pltpu.SemaphoreType.DMA,
         ],
         compiler_params=pltpu.CompilerParams(vmem_limit_bytes=VMEM),
@@ -133,7 +123,7 @@
     )(template_ids, library, channel_mask, station_group.reshape(1, total))
 
 
-def correlate_kernel(unroll, chunk, moved, following, shifts, coef, out, held, tail, phases, inverse, sums, sems, tail_sem):
+def correlate_kernel(unroll, moved, following, held, coef, out, tail, phases, inverse, tail_sem):
     owners, stations, block_len = moved.shape
     width = block_len // PH
     tiles = owners * block_len // (LANES * PH)
@@ -142,12 +132,6 @@
 
     tail_copy = pltpu.make_async_copy(following.at[pl.ds(position * stations, stations)], tail, tail_sem)
     tail_copy.start()
-    loads = [
-        pltpu.make_async_copy(shifts.at[pl.ds(c * chunk, chunk)], held.at[pl.ds(c * chunk, chunk)], sems.at[c])
-        for c in range(stations // chunk)
-    ]
-    for load in loads:
-        load.start()
 
     time = lax.broadcasted_iota(jnp.int32, (W, W), 0)
     place = lax.broadcasted_iota(jnp.int32, (W, W), 1)
@@ -232,9 +216,7 @@
         return tuple(results)
 
     totals = tuple(jnp.zeros((SLOTS, PH, LANES), jnp.float32) for _ in range(tiles))
-    for c, load in enumerate(loads):
-        load.wait()
-        totals = lax.fori_loop(c * chunk, (c + 1) * chunk, station, totals, unroll=unroll)
+    totals = lax.fori_loop(0, stations, station, totals, unroll=unroll)
 
     lane = lane_ids((PH, LANES))
     for d in range(owners):
@@ -252,30 +234,26 @@
 def correlate(moved, following, shifts, coef):
     owners, stations, block_len = moved.shape
     tiles = owners * block_len // (LANES * PH)
-    chunk = min(32, stations)
     return pl.pallas_call(
-        functools.partial(correlate_kernel, 16, chunk),
+        functools.partial(correlate_kernel, 16),
         out_shape=jax.ShapeDtypeStruct((owners, NB, PH, LANES), jnp.float32),
         in_specs=[
             pl.BlockSpec(memory_space=pltpu.VMEM),
             pl.BlockSpec(memory_space=pl.ANY),
-            pl.BlockSpec(memory_space=pl.ANY),
+            pl.BlockSpec(memory_space=pltpu.VMEM),
             pl.BlockSpec(memory_space=pltpu.VMEM),
         ],
         out_specs=pl.BlockSpec(memory_space=pltpu.VMEM),
         scratch_shapes=[
-            pltpu.VMEM(shifts.shape, jnp.bfloat16),
             pltpu.VMEM((stations, following.shape[1]), jnp.bfloat16),
             pltpu.VMEM((tiles + 1, PH * stations, LANES), jnp.float32),
             pltpu.VMEM((tiles, PH * stations, LANES), jnp.float32),
-            pltpu.VMEM((8, LANES), jnp.float32),
-            pltpu.SemaphoreType.DMA((stations // chunk,)),
             pltpu.SemaphoreType.DMA,
         ],
         compiler_params=pltpu.CompilerParams(vmem_limit_bytes=VMEM),
         cost_estimate=pl.CostEstimate(flops=1_200_000_000, bytes_accessed=10_000_000, transcendentals=0),
         name="correlate",
-    )(moved, following, shifts, coef)
+    )(moved, following, pltpu.with_memory_space_constraint(shifts, pltpu.VMEM), pltpu.with_memory_space_constraint(coef, pltpu.VMEM))
 
 
 def finish_kernel(parts, out):

time: 49.9 us -> 54.9 us (1.10)
  local copies, waits for them, and re-layouts: 0.68 us -> 11.6 us
  Pallas kernels: 28.4 us -> 22.6 us
    unnamed x2 -> x14, local copies, waits for them, and re-layouts: 0.68 us -> 11.6 us
    pallas_call x2, Pallas kernels: 26.8 us -> 21.1 us  [the longest x1 11.8 us: correlate(): pl.pallas_call(functools.partial(correlate_kernel, 16), out_shape=jax.Sha...]
  transfers between devices with their start and end apart: 1 -> 1, of which waited for: 0 -> 0; matrix products, arithmetic and copies ran while one was open for 0% -> 0% of each run, Pallas kernels for 22% -> 17%
where the time goes in v2:
time: 54.9 us; the launch traced here: 54.4 us
  Pallas kernels  22.6 us (41%)
  blocking collectives  12.9 us (23%)
  local copies, waits for them, and re-layouts  11.6 us (21%)
  starting transfers between devices  7.28 us (13%)
    all_to_all x1, blocking collectives, shards(): lax.all_to_all(partial_sum.reshape(owners * NB, PH, LANES), ('tm', 'sta')...  12.9 us
    pallas_call x1, Pallas kernels, correlate(): pl.pallas_call(functools.partial(correlate_kernel, 16), out_shape=jax.Sha...  11.8 us
    unnamed x14, local copies, waits for them, and re-layouts  11.6 us
    pallas_call x1, Pallas kernels, prepare(): pl.pallas_call(prepare_kernel, out_shape=(pltpu.VMEM((stations, SLOTS * P...  9.27 us
    all_to_all x1, starting transfers between devices, shards(): lax.all_to_all(records.reshape(owners, stations, block_len), 'tm', split_...  7.28 us
    pallas_call x1, Pallas kernels, finish(): pl.pallas_call(finish_kernel, out_shape=jax.ShapeDtypeStruct((1, KB, LANE...  1.52 us
  transfers between devices with their start and end apart: 1, of which 0 were waited for; matrix products, arithmetic and copies ran while one was open for 0% of the time, Pallas kernels for 17%

profile of v2, /device:TPU:0, one launch (start us, length us, event | category | flops | bytes accessed | tf_op | source)
XLA Modules:
  0.0 54.4 jit_solution(5375586244170562085)
XLA Ops:
  0.0 7.3 %all-to-all-start = ((bf16[8,128,128]{2,1,0:T(8,128)(2,1)}), bf16[8,128,128]{2,1,0:T(8,128)(2,1)S(1)}, u32[]{:S(2)}, u32[]{:S(2)}) async-start(bf16[8,128,128]{2,1,0:T(8,128)(2,1)} %bitcast.5), calls=%async_computation | async-start | bytes 524288 | tf_op jit(solution)/shard_map/all_to_all | solution.py:285
  7.3 0.0 copy-start.2
  7.3 1.6 %copy-done.2 = bf16[32,128,256]{2,1,0:T(8,128)(2,1)S(1)} copy-done((bf16[32,128,256]{2,1,0:T(8,128)(2,1)S(1)}, bf16[32,128,256]{2,1,0:T(8,128)(2,1)}, u32[]{:S(2)}) %copy-start.2) | copy-done | bytes 2097176
  8.9 0.0 copy-start.4
  8.9 0.9 %copy-done.4 = s32[32,2048]{1,0:T(8,128)S(1)} copy-done((s32[32,2048]{1,0:T(8,128)S(1)}, s32[32,2048]{1,0:T(8,128)}, u32[]{:S(2)}) %copy-start.4) | copy-done | bytes 262168
  9.8 0.0 copy-start.5
  9.8 0.7 %copy-done.5 = s32[2048]{0:T(1024)S(1)} copy-done((s32[2048]{0:T(1024)S(1)}, s32[2048]{0:T(1024)}, u32[]{:S(2)}) %copy-start.5) | copy-done | bytes 8216
  10.5 0.0 copy-start.6
  10.5 0.7 %copy-done.6 = s32[2,8]{1,0:T(2,128)S(1)} copy-done((s32[2,8]{1,0:T(2,128)S(1)}, s32[2,8]{1,0:T(2,128)}, u32[]{:S(2)}) %copy-start.6) | copy-done | bytes 88
  11.2 9.3 %prepare.1 = (bf16[128,128,256]{2,1,0:T(8,128)(2,1)S(1)}, f32[2048,128]{1,0:T(8,128)S(1)}) custom-call(s32[2,8]{1,0:T(2,128)S(1)} %copy-done.6, bf16[32,128,256]{2,1,0:T(8,128)(2,1)S(1)} %copy-done.2, s32[32,2048]{1,0:T(8,128)S(1)} %copy-done.4, s32[1,2048]{1,0:T(1,128)S(1)} %bitcast.4), custom_call_target="tpu_custom_call" | custom-call | flops 10000000 | bytes 20000000 | tf_op jit(solution)/shard_map/prepare/pallas_call | solution.py:101
  20.5 0.0 copy-start
  20.5 3.2 %copy-done = bf16[128,128,256]{2,1,0:T(8,128)(2,1)} copy-done((bf16[128,128,256]{2,1,0:T(8,128)(2,1)}, bf16[128,128,256]{2,1,0:T(8,128)(2,1)S(1)}, u32[]{:S(2)}) %copy-start) | copy-done | bytes 8388632
  23.7 0.0 all-to-all-done.moved
  23.7 0.0 copy-start.1
  23.7 3.4 %copy-done.1 = bf16[128,128,256]{2,1,0:T(8,128)(2,1)S(1)} copy-done((bf16[128,128,256]{2,1,0:T(8,128)(2,1)S(1)}, bf16[128,128,256]{2,1,0:T(8,128)(2,1)}, u32[]{:S(2)}) %copy-start.1) | copy-done | bytes 8388632
  27.1 0.0 copy-start.3
  27.1 1.0 %copy-done.3 = bf16[1024,255]{1,0:T(8,128)(2,1)S(1)} copy-done((bf16[1024,255]{1,0:T(8,128)(2,1)S(1)}, bf16[1024,255]{1,0:T(8,128)(2,1)}, u32[]{:S(2)}) %copy-start.3) | copy-done | bytes 522264
  28.1 11.8 %correlate.1 = f32[8,2,8,128]{3,2,1,0:T(8,128)S(1)} custom-call(bf16[8,128,128]{2,1,0:T(8,128)(2,1)S(1)} %all-to-all-done.moved, bf16[1024,255]{1,0:T(8,128)(2,1)S(1)} %copy-done.3, bf16[128,128,256]{2,1,0:T(8,128)(2,1)S(1)} %copy-done.1, f32[2048,128]{1,0:T(8,128)S(1)} %get-tuple-element.8.coef), custom_call_target="tpu_custom_call" | custom-call | flops 1200000000 | bytes 10000000 | tf_op jit(solution)/shard_map/correlate/pallas_call | solution.py:237
  40.0 12.9 %all_to_all.10.parts = f32[16,8,128]{2,1,0:T(8,128)} all-to-all(f32[16,8,128]{2,1,0:T(8,128)S(1)} %bitcast.3), channel_id=1, replica_groups=mesh['days'=2,'tm'=8,'sta'=2] {'tm','sta'}, dimensions={0} | all-to-all | bytes 131072 | tf_op jit(solution)/shard_map/all_to_all | solution.py:288
  52.9 1.5 %finish.1 = f32[1,8,128]{2,1,0:T(8,128)} custom-call(f32[16,8,128]{2,1,0:T(8,128)} %all_to_all.10.parts), custom_call_target="tpu_custom_call" | custom-call | tf_op jit(solution)/shard_map/finish/pallas_call | solution.py:272
Async XLA Ops:
  0.0 23.7 %all-to-all-start = ((bf16[8,128,128]{2,1,0:T(8,128)(2,1)}), bf16[8,128,128]{2,1,0:T(8,128)(2,1)S(1)}, u32[]{:S(2)}, u32[]{:S(2)}) async-start(bf16[8,128,128]{2,1,0:T(8,128)(2,1)} %bitcast.5), calls=%async_computation | async-start | bytes 524288 | tf_op jit(solution)/shard_map/all_to_all | solution.py:285
  7.3 1.6 %copy-start.2 = (bf16[32,128,256]{2,1,0:T(8,128)(2,1)S(1)}, bf16[32,128,256]{2,1,0:T(8,128)(2,1)}, u32[]{:S(2)}) copy-start(bf16[32,128,256]{2,1,0:T(8,128)(2,1)} %library.1) | copy-start | bytes 6291460
  8.9 0.9 %copy-start.4 = (s32[32,2048]{1,0:T(8,128)S(1)}, s32[32,2048]{1,0:T(8,128)}, u32[]{:S(2)}) copy-start(s32[32,2048]{1,0:T(8,128)} %mask.1) | copy-start | bytes 786436
  9.8 0.7 %copy-start.5 = (s32[2048]{0:T(1024)S(1)}, s32[2048]{0:T(1024)}, u32[]{:S(2)}) copy-start(s32[2048]{0:T(1024)} %param.11) | copy-start | bytes 24580
  10.5 0.7 %copy-start.6 = (s32[2,8]{1,0:T(2,128)S(1)}, s32[2,8]{1,0:T(2,128)}, u32[]{:S(2)}) copy-start(s32[2,8]{1,0:T(2,128)} %ids.1) | copy-start | bytes 196
  20.5 3.2 %copy-start = (bf16[128,128,256]{2,1,0:T(8,128)(2,1)}, bf16[128,128,256]{2,1,0:T(8,128)(2,1)S(1)}, u32[]{:S(2)}) copy-start(bf16[128,128,256]{2,1,0:T(8,128)(2,1)S(1)} %get-tuple-element.7.held) | copy-start | bytes 25165828
  23.7 3.4 %copy-start.1 = (bf16[128,128,256]{2,1,0:T(8,128)(2,1)S(1)}, bf16[128,128,256]{2,1,0:T(8,128)(2,1)}, u32[]{:S(2)}) copy-start(bf16[128,128,256]{2,1,0:T(8,128)(2,1)} %copy-done) | copy-start | bytes 25165828
  27.1 1.0 %copy-start.3 = (bf16[1024,255]{1,0:T(8,128)(2,1)S(1)}, bf16[1024,255]{1,0:T(8,128)(2,1)}, u32[]{:S(2)}) copy-start(bf16[1024,255]{1,0:T(8,128)(2,1)} %following.1) | copy-start | bytes 1566724

commit v3 on v1

v3 whole, which is shorter than its diff:
```python
import functools
import math

import jax
import jax.numpy as jnp
from jax import lax
from jax.experimental import pallas as pl
from jax.experimental.pallas import tpu as pltpu
from jax.sharding import PartitionSpec as P

W = 256
NB = 2
KB = 8
G = 128
SLOTS = NB * KB
PH = 8
LANES = 128
TAPS = W // PH
PIECES = LANES // TAPS
VMEM = 24 << 20
CHUNK = 64

epsilon = 1e-06


def lane_ids(shape):
    return lax.broadcasted_iota(jnp.int32, shape, len(shape) - 1)


def shifted(here, after, by):
    if by == 0:
        return here
    lane = lane_ids(here.shape)
    return pltpu.roll(jnp.where(lane < by, after, here), LANES - by, here.ndim - 1)


def swap_groups(values, width):
    lane = lane_ids(values[0].shape)
    step = len(values) // 2
    while step:
        values = list(values)
        low = lane // (width * step) % 2 == 0
        for q in range(len(values)):
            if q // step % 2 == 0:
                a, b = values[q], values[q + step]
                values[q] = jnp.where(low, a, pltpu.roll(b, width * step, b.ndim - 1))
                values[q + step] = jnp.where(low, pltpu.roll(a, LANES - width * step, a.ndim - 1), b)
        step //= 2
    return values


def prepare_kernel(chunk, ids, library, mask, group, shifts, coef, picked, wide, rows, made, gains, row_sem, in_sem, out_sem, gain_sem):
    stations = library.shape[1]
    total = mask.shape[1]
    for k in range(SLOTS):
        pltpu.make_async_copy(mask.at[pl.ds(ids[k // KB, k % KB], 1)], rows.at[pl.ds(k, 1)], row_sem).start()
    for k in range(SLOTS):
        pltpu.make_async_copy(library.at[ids[k // KB, k % KB]], picked.at[k], in_sem).start()
    pltpu.make_async_copy(mask.at[pl.ds(0, SLOTS)], rows, row_sem).wait()

    members = lax.broadcasted_iota(jnp.int32, (G, total), 0) == group[...]
    counts = lax.dot_general(
        rows[...].astype(jnp.float32).astype(jnp.bfloat16),
        members.astype(jnp.float32).astype(jnp.bfloat16),
        (((1,), (1,)), ((), ())),
        preferred_element_type=jnp.float32,
    )
    first = lax.axis_index("sta") * (stations * lax.axis_size("tm")) + lax.axis_index("tm") * stations
    block = pl.multiple_of(first // LANES * LANES, LANES)
    own_group = jnp.broadcast_to(group[:, pl.ds(block, LANES)], (G, LANES))
    own_mask = rows[:, pl.ds(block, LANES)].astype(jnp.float32)
    own = (lax.broadcasted_iota(jnp.int32, (G, LANES), 0) == own_group).astype(jnp.float32)
    per_station = jnp.dot(counts, own, preferred_element_type=jnp.float32, precision=lax.Precision.HIGHEST)
    scaled = own_mask / jnp.sqrt(jnp.float32(W * G) * jnp.maximum(per_station, 1.0))
    if stations % LANES:
        scaled = pltpu.roll(scaled, LANES - (first - block), 1)
    scaled = jnp.concatenate([scaled, jnp.zeros((LANES - SLOTS, LANES), jnp.float32)], axis=0).T

    for k in range(SLOTS):
        pltpu.make_async_copy(library.at[0], picked.at[k], in_sem).wait()
    columns = []
    for k in range(SLOTS):
        values = picked[k].astype(jnp.float32)
        wide[k] = values
        tmean = jnp.sum(values * values, axis=1, keepdims=True) / W
        value = scaled[:stations, k : k + 1] / jnp.sqrt(tmean + epsilon)
        columns.append(jnp.broadcast_to(value, (stations, LANES)))
    gains[...] = jnp.swapaxes(jnp.stack(columns), 0, 1)
    gains_out = pltpu.make_async_copy(gains, coef, gain_sem)
    gains_out.start()

    lane = lane_ids((PH, LANES))
    row = lax.broadcasted_iota(jnp.int32, (PH, LANES), 0)
    inside = lane >= row

    def station(s):
        for pair in range(SLOTS // 2):
            halves = []
            for k in (2 * pair, 2 * pair + 1):
                template = wide[k, pl.ds(s, 1), :]
                turned = [
                    pltpu.roll(
                        jnp.broadcast_to(template[:, h * LANES : (h + 1) * LANES], (PH, LANES)), 0, 1, stride=1, stride_axis=0
                    )
                    for h in range(W // LANES)
                ]
                halves.append(
                    jnp.concatenate(
                        [jnp.where(inside, turned[h], turned[h - 1]) for h in range(W // LANES)], axis=1
                    )
                )
            made[s, 2 * PH * pair : 2 * PH * (pair + 1), :] = jnp.concatenate(halves, axis=0).astype(jnp.bfloat16)

    def part(c, carry):
        def step(i, inner):
            station(c * chunk + i)
            return inner

        lax.fori_loop(0, chunk, step, 0, unroll=True)
        span = pl.ds(c * chunk, chunk)
        pltpu.make_async_copy(made.at[span], shifts.at[span], out_sem).start()
        return carry

    lax.fori_loop(0, stations // chunk, part, 0)
    gains_out.wait()
    pltpu.make_async_copy(made, shifts, out_sem).wait()


def prepare(template_ids, library, channel_mask, station_group):
    stations = library.shape[1]
    total = channel_mask.shape[1]
    chunk = min(16, stations)
    return pl.pallas_call(
        functools.partial(prepare_kernel, chunk),
        out_shape=(
            pltpu.HBM((stations, SLOTS * PH, W), jnp.bfloat16),
            pltpu.HBM((stations, SLOTS, LANES), jnp.float32),
        ),
        in_specs=[
            pl.BlockSpec(memory_space=pltpu.SMEM),
            pl.BlockSpec(memory_space=pl.ANY),
            pl.BlockSpec(memory_space=pl.ANY),
            pl.BlockSpec(memory_space=pltpu.VMEM),
        ],
        out_specs=(pl.BlockSpec(memory_space=pl.ANY), pl.BlockSpec(memory_space=pl.ANY)),
        scratch_shapes=[
            pltpu.VMEM((SLOTS, stations, W), jnp.bfloat16),
            pltpu.VMEM((SLOTS, stations, W), jnp.float32),
            pltpu.VMEM((SLOTS, total), jnp.int32),
            pltpu.VMEM((stations, SLOTS * PH, W), jnp.bfloat16),
            pltpu.VMEM((stations, SLOTS, LANES), jnp.float32),
            pltpu.SemaphoreType.DMA,
            pltpu.SemaphoreType.DMA,
            pltpu.SemaphoreType.DMA,
            pltpu.SemaphoreType.DMA,
        ],
        compiler_params=pltpu.CompilerParams(vmem_limit_bytes=VMEM),
        cost_estimate=pl.CostEstimate(flops=10_000_000, bytes_accessed=20_000_000, transcendentals=0),
        name="prepare",
    )(
        template_ids,
        *(pltpu.with_memory_space_constraint(v, pltpu.HBM) for v in (library, channel_mask, station_group.reshape(1, total))),
    )


def correlate_kernel(chunk, moved, following, shifts, coef, out, held, gains, tail, phases, inverse, held_sems, gain_sem, tail_sem):
    owners, stations, block_len = moved.shape
    width = block_len // PH
    tiles = owners * block_len // (LANES * PH)
    per_tile = LANES // width
    position = lax.axis_index("tm")

    tail_copy = pltpu.make_async_copy(following.at[pl.ds(position * stations, stations)], tail, tail_sem)
    tail_copy.start()
    held_copies = [
        pltpu.make_async_copy(shifts.at[pl.ds(c, chunk)], held.at[pl.ds(c, chunk)], held_sems.at[c // chunk])
        for c in range(0, stations, chunk)
    ]
    held_copies[0].start()
    gain_copy = pltpu.make_async_copy(coef, gains, gain_sem)
    gain_copy.start()
    for copy in held_copies[1:]:
        copy.start()

    time = lax.broadcasted_iota(jnp.int32, (W, W), 0)
    place = lax.broadcasted_iota(jnp.int32, (W, W), 1)
    sample = place % TAPS * PH + place // TAPS
    order = (time == sample).astype(jnp.float32).astype(jnp.bfloat16)
    here = (time >= sample).astype(jnp.float32).astype(jnp.bfloat16)
    beyond = (time < sample).astype(jnp.float32).astype(jnp.bfloat16)

    def squares(rows):
        value = jnp.square(rows.astype(jnp.float32))
        high = value.astype(jnp.bfloat16)
        return high, (value - high.astype(jnp.float32)).astype(jnp.bfloat16)

    def spread(target, j, split):
        parts = []
        for half in range(PH // PIECES):
            parts += swap_groups([v[:, half * LANES : (half + 1) * LANES] for v in split], TAPS)
        target[j] = jnp.swapaxes(jnp.stack(parts), 0, 1)

    each = W // block_len
    rows = [
        jnp.concatenate([moved[q * each + e] for e in range(each)], axis=1) for q in range(tiles * PIECES)
    ]
    for j in range(tiles):
        spread(
            phases,
            j,
            [jnp.dot(rows[j * PIECES + q], order, preferred_element_type=jnp.float32) for q in range(PIECES)],
        )
    tail_copy.wait()
    rows.append(jnp.concatenate([tail[...], jnp.zeros((stations, 1), jnp.bfloat16)], axis=1))
    split = jnp.dot(rows[-1], order, preferred_element_type=jnp.float32)
    parts = []
    for p in range(PH):
        half, at = p // PIECES, p % PIECES
        piece = split[:, half * LANES : (half + 1) * LANES]
        parts.append(pltpu.roll(piece, (-TAPS * at) % LANES, 1) if at else piece)
    phases[tiles] = jnp.swapaxes(jnp.stack(parts), 0, 1)

    squared = [squares(r) for r in rows]
    for j in range(tiles):
        split = []
        for q in range(j * PIECES, (j + 1) * PIECES):
            energy = sum(
                jnp.dot(part, matrix, preferred_element_type=jnp.float32)
                for parts, matrix in ((squared[q], here), (squared[q + 1], beyond))
                for part in parts
            )
            split.append(lax.rsqrt(energy / W + epsilon))
        spread(inverse, j, split)

    row = lax.broadcasted_iota(jnp.int32, (2 * PH, LANES), 0) % PH
    inside = (lane_ids((2 * PH, LANES)) >= row).astype(jnp.float32).astype(jnp.bfloat16)

    def station(s, totals):
        templates = held[s]
        head = templates[:, :LANES].reshape(SLOTS // 2, 2 * PH, LANES)
        kept = head * inside[None]
        rest = (head - kept).reshape(SLOTS * PH, LANES)[:, : 2 * PH]
        main = jnp.concatenate([kept.reshape(SLOTS * PH, LANES), templates[:, LANES:], rest], axis=1)
        gain = gains[s]
        own = [phases[j, s] for j in range(tiles + 1)]
        results = []
        for j in range(tiles):
            window = [shifted(own[j], own[j + 1], by) for by in range(TAPS + 1)]
            window.append(jnp.zeros_like(own[j]))
            pairs = [
                jnp.concatenate(window[2 * i : 2 * i + 2], axis=0).astype(jnp.bfloat16) for i in range(TAPS // 2 + 1)
            ]
            corr = jnp.dot(main, jnp.concatenate(pairs, axis=0), preferred_element_type=jnp.float32)
            scale = inverse[j, s]
            results.append(totals[j] + (corr.reshape(SLOTS, PH, LANES) * scale[None]) * gain[:, None, :])
        return tuple(results)

    totals = tuple(jnp.zeros((SLOTS, PH, LANES), jnp.float32) for _ in range(tiles))
    gain_copy.wait()

    def part(c, totals):
        span = pl.ds(c * chunk, chunk)
        pltpu.make_async_copy(shifts.at[span], held.at[span], held_sems.at[c]).wait()
        return lax.fori_loop(0, chunk, lambda i, totals: station(c * chunk + i, totals), totals, unroll=True)

    totals = lax.fori_loop(0, stations // chunk, part, totals)

    lane = lane_ids((KB, LANES))
    source = lax.broadcasted_iota(jnp.int32, (KB, LANES), 0) * width + lane // PH
    for j in range(tiles):
        for b in range(NB):
            tile = swap_groups([totals[j][b * KB + k] for k in range(KB)], width)
            for at in range(per_tile):
                value = None
                for p in range(PH):
                    one = jnp.broadcast_to(tile[at][p : p + 1, :], (KB, LANES))
                    one = jnp.take_along_axis(one, source, axis=1)
                    value = one if value is None else jnp.where(lane % PH == p, one, value)
                out[j * per_tile + at, b] = value


def correlate(moved, following, shifts, coef):
    owners, stations, block_len = moved.shape
    tiles = owners * block_len // (LANES * PH)
    chunk = math.gcd(stations, CHUNK)
    return pl.pallas_call(
        functools.partial(correlate_kernel, chunk),
        out_shape=jax.ShapeDtypeStruct((owners, NB, KB, LANES), jnp.float32),
        in_specs=[
            pl.BlockSpec(memory_space=pltpu.VMEM),
            pl.BlockSpec(memory_space=pl.ANY),
            pl.BlockSpec(memory_space=pl.ANY),
            pl.BlockSpec(memory_space=pl.ANY),
        ],
        out_specs=pl.BlockSpec(memory_space=pltpu.VMEM),
        scratch_shapes=[
            pltpu.VMEM(shifts.shape, jnp.bfloat16),
            pltpu.VMEM(coef.shape, jnp.float32),
            pltpu.VMEM((stations, following.shape[1]), jnp.bfloat16),
            pltpu.VMEM((tiles + 1, stations, PH, LANES), jnp.float32),
            pltpu.VMEM((tiles, stations, PH, LANES), jnp.float32),
            pltpu.SemaphoreType.DMA((stations // chunk,)),
            pltpu.SemaphoreType.DMA,
            pltpu.SemaphoreType.DMA,
        ],
        compiler_params=pltpu.CompilerParams(vmem_limit_bytes=VMEM),
        cost_estimate=pl.CostEstimate(flops=1_200_000_000, bytes_accessed=10_000_000, transcendentals=0),
        name="correlate",
    )(moved, *(pltpu.with_memory_space_constraint(v, pltpu.HBM) for v in (following, shifts, coef)))


def shards(records, following, library, template_ids, channel_mask, station_group):
    owners = lax.axis_size("tm")
    block_len = records.shape[1]
    stations = library.shape[1]
    moved = lax.all_to_all(records.reshape(owners, stations, block_len), "tm", split_axis=0, concat_axis=0)
    shifts, coef = prepare(template_ids, library, channel_mask, station_group)
    partial_sum = correlate(moved, following, shifts, coef)
    parts = lax.all_to_all(
        partial_sum.reshape(owners * NB, KB, block_len), ("tm", "sta"), split_axis=0, concat_axis=0
    )
    return jnp.sum(parts, axis=0)[None]


def solution(mesh):
    placed = (
        P("sta", ("days", "tm")),
        P("sta", "days"),
        P(None, ("sta", "tm"), None),
        P(),
        P(),
        P(),
    )
    return jax.shard_map(
        shards,
        mesh=mesh,
        in_specs=placed,
        out_specs=P("sta", None, ("days", "tm")),
        check_vma=False,
    )
```

time: 49.9 us -> 37.8 us (0.76)
  Pallas kernels: 28.4 us -> 16 us
  blocking collectives: 13.1 us -> 11.6 us
  waiting for transfers between devices: 0.01 us -> 1.19 us
  other arithmetic: 0 us -> 0.61 us
    pallas_call x3 -> x2, Pallas kernels: 28.4 us -> 16 us  [the longest x1 8.94 us: correlate(): pl.pallas_call(functools.partial(correlate_kernel, chunk), out_shape=jax....]
    all_to_all x1, blocking collectives: 13.1 us -> 11.6 us  [shards(): lax.all_to_all(partial_sum.reshape(owners * NB, KB, block_len), ('tm', 's...]
    all_to_all x1, waiting for transfers between devices: 0.01 us -> 1.19 us  [shards(): lax.all_to_all(records.reshape(owners, stations, block_len), 'tm', split_...]
    reduce_sum x0 -> x1, other arithmetic: none -> 0.61 us  [shards(): return jnp.sum(parts, axis=0)[None]]
  transfers between devices with their start and end apart: 1 -> 1, of which waited for: 0 -> 1; matrix products, arithmetic and copies ran while one was open for 0% -> 0% of each run, Pallas kernels for 22% -> 19%
where the time goes in v3:
time: 37.8 us; the launch traced here: 37.4 us
  Pallas kernels  16 us (42%)
  blocking collectives  11.6 us (31%)
  starting transfers between devices  7.28 us (19%)
  waiting for transfers between devices  1.19 us (3%)
  local copies, waits for them, and re-layouts  0.68 us (2%)
  other arithmetic  0.61 us (2%)
    all_to_all x1, blocking collectives, shards(): lax.all_to_all(partial_sum.reshape(owners * NB, KB, block_len), ('tm', 's...  11.6 us
    pallas_call x1, Pallas kernels, correlate(): pl.pallas_call(functools.partial(correlate_kernel, chunk), out_shape=jax....  8.94 us
    all_to_all x1, starting transfers between devices, shards(): lax.all_to_all(records.reshape(owners, stations, block_len), 'tm', split_...  7.28 us
    pallas_call x1, Pallas kernels, prepare(): pl.pallas_call(functools.partial(prepare_kernel, chunk), out_shape=(pltpu...  7.04 us
    all_to_all x1, waiting for transfers between devices, shards(): lax.all_to_all(records.reshape(owners, stations, block_len), 'tm', split_...  1.19 us
  transfers between devices with their start and end apart: 1, of which 1 were waited for; matrix products, arithmetic and copies ran while one was open for 0% of the time, Pallas kernels for 19%

profile of v3, /device:TPU:0, one launch (start us, length us, event | category | flops | bytes accessed | tf_op | source)
XLA Modules:
  0.0 37.4 jit_solution(16686320105924534522)
XLA Ops:
  0.0 7.3 %all-to-all-start = ((bf16[8,128,128]{2,1,0:T(8,128)(2,1)}), bf16[8,128,128]{2,1,0:T(8,128)(2,1)S(1)}, u32[]{:S(2)}, u32[]{:S(2)}) async-start(bf16[8,128,128]{2,1,0:T(8,128)(2,1)} %bitcast.5), calls=%async_computation | async-start | bytes 524288 | tf_op jit(solution)/shard_map/all_to_all | solution.py:316
  7.3 0.0 copy-start
  7.3 0.7 %copy-done = s32[2,8]{1,0:T(2,128)S(1)} copy-done((s32[2,8]{1,0:T(2,128)S(1)}, s32[2,8]{1,0:T(2,128)}, u32[]{:S(2)}) %copy-start) | copy-done | bytes 88
  8.0 7.0 %prepare.1 = (bf16[128,128,256]{2,1,0:T(8,128)(2,1)}, f32[128,16,128]{2,1,0:T(8,128)}) custom-call(s32[2,8]{1,0:T(2,128)S(1)} %copy-done, bf16[32,128,256]{2,1,0:T(8,128)(2,1)} %library.1, s32[32,2048]{1,0:T(8,128)} %mask.1, s32[1,2048]{1,0:T(1,128)} %bitcast.6), custom_call_target="tpu_custom_call" | custom-call | flops 10000000 | bytes 20000000 | tf_op jit(solution)/shard_map/prepare/pallas_call | solution.py:133
  15.0 1.2 %all-to-all-done.moved = bf16[8,128,128]{2,1,0:T(8,128)(2,1)S(1)} async-done(((bf16[8,128,128]{2,1,0:T(8,128)(2,1)}), bf16[8,128,128]{2,1,0:T(8,128)(2,1)S(1)}, u32[]{:S(2)}, u32[]{:S(2)}) %all-to-all-start) | async-done | bytes 262176 | tf_op jit(solution)/shard_map/all_to_all | solution.py:316
  16.2 8.9 %correlate.1 = f32[8,2,8,128]{3,2,1,0:T(8,128)S(1)} custom-call(bf16[8,128,128]{2,1,0:T(8,128)(2,1)S(1)} %all-to-all-done.moved, bf16[1024,255]{1,0:T(8,128)(2,1)} %following.1, bf16[128,128,256]{2,1,0:T(8,128)(2,1)} %get-tuple-element.7.shifts, f32[128,16,128]{2,1,0:T(8,128)} %get-tuple-element.8.coef), custom_call_target="tpu_custom_call" | custom-call | flops 1200000000 | bytes 10000000 | tf_op jit(solution)/shard_map/correlate/pallas_call | solution.py:286
  25.2 11.6 %all_to_all.10 = f32[16,8,128]{2,1,0:T(8,128)S(1)} all-to-all(f32[16,8,128]{2,1,0:T(8,128)S(1)} %bitcast.4), channel_id=1, replica_groups=mesh['days'=2,'tm'=8,'sta'=2] {'tm','sta'}, dimensions={0} | all-to-all | bytes 131072 | tf_op jit(solution)/shard_map/all_to_all | solution.py:319
  36.8 0.6 %reduce_sum.9 = f32[8,128]{1,0:T(8,128)} reduce(f32[16,8,128]{2,1,0:T(8,128)S(1)} %all_to_all.10, f32[]{:T(128)} %constant.0.clone.1), dimensions={0}, to_apply=%region_0.0 | reduce | flops 15360 | bytes 69636 | tf_op jit(solution)/shard_map/reduce_sum | solution.py:322
Async XLA Ops:
  0.0 16.2 %all-to-all-start = ((bf16[8,128,128]{2,1,0:T(8,128)(2,1)}), bf16[8,128,128]{2,1,0:T(8,128)(2,1)S(1)}, u32[]{:S(2)}, u32[]{:S(2)}) async-start(bf16[8,128,128]{2,1,0:T(8,128)(2,1)} %bitcast.5), calls=%async_computation | async-start | bytes 524288 | tf_op jit(solution)/shard_map/all_to_all | solution.py:316
  7.3 0.7 %copy-start = (s32[2,8]{1,0:T(2,128)S(1)}, s32[2,8]{1,0:T(2,128)}, u32[]{:S(2)}) copy-start(s32[2,8]{1,0:T(2,128)} %ids.1) | copy-start | bytes 196

commit v4 on v3

--- a/solution.py
+++ b/solution.py
@@ -39,7 +39,8 @@
     step = len(values) // 2
     while step:
         values = list(values)
-        low = lane // (width * step) % 2 == 0
+        low = lane // (width * step) % 2
+        low = (low if values[0].dtype == jnp.float32 else low.astype(jnp.float32).astype(values[0].dtype)) == 0
         for q in range(len(values)):
             if q // step % 2 == 0:
                 a, b = values[q], values[q + step]
@@ -49,23 +50,50 @@
     return values
 
 
-def prepare_kernel(chunk, ids, library, mask, group, shifts, coef, picked, wide, rows, made, gains, row_sem, in_sem, out_sem, gain_sem):
+def prepare_kernel(
+    chunk,
+    ids,
+    library,
+    mask,
+    group,
+    following,
+    shifts,
+    coef,
+    after,
+    picked,
+    wide,
+    rows,
+    made,
+    gains,
+    own_tail,
+    tail,
+    row_sem,
+    in_sem,
+    tail_sem,
+    out_sem,
+    gain_sem,
+    after_sem,
+):
     stations = library.shape[1]
     total = mask.shape[1]
+    position = lax.axis_index("tm")
     for k in range(SLOTS):
         pltpu.make_async_copy(mask.at[pl.ds(ids[k // KB, k % KB], 1)], rows.at[pl.ds(k, 1)], row_sem).start()
     for k in range(SLOTS):
         pltpu.make_async_copy(library.at[ids[k // KB, k % KB]], picked.at[k], in_sem).start()
+    tail_in = pltpu.make_async_copy(following.at[pl.ds(position * stations, stations)], own_tail, tail_sem)
+    tail_in.start()
+
+    members = lax.broadcasted_iota(jnp.int32, (G, total), 0) == group[...]
+    members = members.astype(jnp.float32).astype(jnp.bfloat16)
     pltpu.make_async_copy(mask.at[pl.ds(0, SLOTS)], rows, row_sem).wait()
-
-    members = lax.broadcasted_iota(jnp.int32, (G, total), 0) == group[...]
     counts = lax.dot_general(
         rows[...].astype(jnp.float32).astype(jnp.bfloat16),
-        members.astype(jnp.float32).astype(jnp.bfloat16),
+        members,
         (((1,), (1,)), ((), ())),
         preferred_element_type=jnp.float32,
     )
-    first = lax.axis_index("sta") * (stations * lax.axis_size("tm")) + lax.axis_index("tm") * stations
+    first = lax.axis_index("sta") * (stations * lax.axis_size("tm")) + position * stations
     block = pl.multiple_of(first // LANES * LANES, LANES)
     own_group = jnp.broadcast_to(group[:, pl.ds(block, LANES)], (G, LANES))
     own_mask = rows[:, pl.ds(block, LANES)].astype(jnp.float32)
@@ -88,6 +116,10 @@
     gains[...] = jnp.swapaxes(jnp.stack(columns), 0, 1)
     gains_out = pltpu.make_async_copy(gains, coef, gain_sem)
     gains_out.start()
+    tail_in.wait()
+    tail[...] = jnp.concatenate([own_tail[...], jnp.zeros((stations, 1), jnp.bfloat16)], axis=1)
+    tail_out = pltpu.make_async_copy(tail, after, after_sem)
+    tail_out.start()
 
     lane = lane_ids((PH, LANES))
     row = lax.broadcasted_iota(jnp.int32, (PH, LANES), 0)
@@ -123,44 +155,44 @@
 
     lax.fori_loop(0, stations // chunk, part, 0)
     gains_out.wait()
+    tail_out.wait()
     pltpu.make_async_copy(made, shifts, out_sem).wait()
 
 
-def prepare(template_ids, library, channel_mask, station_group):
+def prepare(template_ids, library, channel_mask, station_group, following):
     stations = library.shape[1]
     total = channel_mask.shape[1]
     chunk = min(16, stations)
+    inputs = template_ids, library, channel_mask, station_group.reshape(1, total), following
     return pl.pallas_call(
         functools.partial(prepare_kernel, chunk),
         out_shape=(
             pltpu.HBM((stations, SLOTS * PH, W), jnp.bfloat16),
             pltpu.HBM((stations, SLOTS, LANES), jnp.float32),
+            pltpu.HBM((stations, W), jnp.bfloat16),
         ),
         in_specs=[
             pl.BlockSpec(memory_space=pltpu.SMEM),
             pl.BlockSpec(memory_space=pl.ANY),
             pl.BlockSpec(memory_space=pl.ANY),
             pl.BlockSpec(memory_space=pltpu.VMEM),
+            pl.BlockSpec(memory_space=pl.ANY),
         ],
-        out_specs=(pl.BlockSpec(memory_space=pl.ANY), pl.BlockSpec(memory_space=pl.ANY)),
+        out_specs=[pl.BlockSpec(memory_space=pl.ANY)] * 3,
         scratch_shapes=[
             pltpu.VMEM((SLOTS, stations, W), jnp.bfloat16),
             pltpu.VMEM((SLOTS, stations, W), jnp.float32),
             pltpu.VMEM((SLOTS, total), jnp.int32),
             pltpu.VMEM((stations, SLOTS * PH, W), jnp.bfloat16),
             pltpu.VMEM((stations, SLOTS, LANES), jnp.float32),
-            pltpu.SemaphoreType.DMA,
-            pltpu.SemaphoreType.DMA,
-            pltpu.SemaphoreType.DMA,
-            pltpu.SemaphoreType.DMA,
-        ],
+            pltpu.VMEM((stations, following.shape[1]), jnp.bfloat16),
+            pltpu.VMEM((stations, W), jnp.bfloat16),
+        ]
+        + [pltpu.SemaphoreType.DMA] * 6,
         compiler_params=pltpu.CompilerParams(vmem_limit_bytes=VMEM),
         cost_estimate=pl.CostEstimate(flops=10_000_000, bytes_accessed=20_000_000, transcendentals=0),
         name="prepare",
-    )(
-        template_ids,
-        *(pltpu.with_memory_space_constraint(v, pltpu.HBM) for v in (library, channel_mask, station_group.reshape(1, total))),
-    )
+    )(*(pltpu.with_memory_space_constraint(v, pltpu.HBM) for v in inputs))
 
 
 def correlate_kernel(chunk, moved, following, shifts, coef, out, held, gains, tail, phases, inverse, held_sems, gain_sem, tail_sem):
@@ -168,9 +200,8 @@
     width = block_len // PH
     tiles = owners * block_len // (LANES * PH)
     per_tile = LANES // width
-    position = lax.axis_index("tm")
-
-    tail_copy = pltpu.make_async_copy(following.at[pl.ds(position * stations, stations)], tail, tail_sem)
+
+    tail_copy = pltpu.make_async_copy(following, tail, tail_sem)
     tail_copy.start()
     held_copies = [
         pltpu.make_async_copy(shifts.at[pl.ds(c, chunk)], held.at[pl.ds(c, chunk)], held_sems.at[c // chunk])
@@ -184,53 +215,55 @@
 
     time = lax.broadcasted_iota(jnp.int32, (W, W), 0)
     place = lax.broadcasted_iota(jnp.int32, (W, W), 1)
-    sample = place % TAPS * PH + place // TAPS
-    order = (time == sample).astype(jnp.float32).astype(jnp.bfloat16)
-    here = (time >= sample).astype(jnp.float32).astype(jnp.bfloat16)
-    beyond = (time < sample).astype(jnp.float32).astype(jnp.bfloat16)
+    order = (time == place % TAPS * PH + place // TAPS).astype(jnp.float32).astype(jnp.bfloat16)
+
+    def split(rows):
+        value = jnp.dot(rows, order, preferred_element_type=jnp.float32).astype(jnp.bfloat16)
+        return [value[:, h * LANES : (h + 1) * LANES] for h in range(W // LANES)]
+
+    def keep(target, j, parts):
+        parts = jnp.stack([v.astype(jnp.float32) for v in parts])
+        target[j] = jnp.swapaxes(parts, 0, 1)
+
+    here = (time >= place % TAPS * PH + place // TAPS).astype(jnp.float32).astype(jnp.bfloat16)
+    beyond = (time < place % TAPS * PH + place // TAPS).astype(jnp.float32).astype(jnp.bfloat16)
 
     def squares(rows):
         value = jnp.square(rows.astype(jnp.float32))
         high = value.astype(jnp.bfloat16)
         return high, (value - high.astype(jnp.float32)).astype(jnp.bfloat16)
-
-    def spread(target, j, split):
-        parts = []
-        for half in range(PH // PIECES):
-            parts += swap_groups([v[:, half * LANES : (half + 1) * LANES] for v in split], TAPS)
-        target[j] = jnp.swapaxes(jnp.stack(parts), 0, 1)
 
     each = W // block_len
     rows = [
         jnp.concatenate([moved[q * each + e] for e in range(each)], axis=1) for q in range(tiles * PIECES)
     ]
     for j in range(tiles):
-        spread(
-            phases,
-            j,
-            [jnp.dot(rows[j * PIECES + q], order, preferred_element_type=jnp.float32) for q in range(PIECES)],
-        )
+        pieces = [split(r) for r in rows[j * PIECES : (j + 1) * PIECES]]
+        keep(phases, j, [v for h in range(PH // PIECES) for v in swap_groups([p[h] for p in pieces], TAPS)])
     tail_copy.wait()
-    rows.append(jnp.concatenate([tail[...], jnp.zeros((stations, 1), jnp.bfloat16)], axis=1))
-    split = jnp.dot(rows[-1], order, preferred_element_type=jnp.float32)
-    parts = []
-    for p in range(PH):
-        half, at = p // PIECES, p % PIECES
-        piece = split[:, half * LANES : (half + 1) * LANES]
-        parts.append(pltpu.roll(piece, (-TAPS * at) % LANES, 1) if at else piece)
-    phases[tiles] = jnp.swapaxes(jnp.stack(parts), 0, 1)
+    rows.append(tail[...])
+    last = split(rows[-1])
+    keep(
+        phases,
+        tiles,
+        [
+            pltpu.roll(last[p // PIECES], LANES - TAPS * (p % PIECES), 1) if p % PIECES else last[p // PIECES]
+            for p in range(PH)
+        ],
+    )
 
     squared = [squares(r) for r in rows]
     for j in range(tiles):
-        split = []
+        pieces = []
         for q in range(j * PIECES, (j + 1) * PIECES):
             energy = sum(
                 jnp.dot(part, matrix, preferred_element_type=jnp.float32)
                 for parts, matrix in ((squared[q], here), (squared[q + 1], beyond))
                 for part in parts
             )
-            split.append(lax.rsqrt(energy / W + epsilon))
-        spread(inverse, j, split)
+            energy = lax.rsqrt(energy / W + epsilon)
+            pieces.append([energy[:, h * LANES : (h + 1) * LANES] for h in range(W // LANES)])
+        keep(inverse, j, [v for h in range(PH // PIECES) for v in swap_groups([p[h] for p in pieces], TAPS)])
 
     row = lax.broadcasted_iota(jnp.int32, (2 * PH, LANES), 0) % PH
     inside = (lane_ids((2 * PH, LANES)) >= row).astype(jnp.float32).astype(jnp.bfloat16)
@@ -241,7 +274,7 @@
         kept = head * inside[None]
         rest = (head - kept).reshape(SLOTS * PH, LANES)[:, : 2 * PH]
         main = jnp.concatenate([kept.reshape(SLOTS * PH, LANES), templates[:, LANES:], rest], axis=1)
-        gain = gains[s]
+        gain = [jnp.broadcast_to(gains[s, pl.ds(k, 1), :], (PH, LANES)) for k in range(SLOTS)]
         own = [phases[j, s] for j in range(tiles + 1)]
         results = []
         for j in range(tiles):
@@ -252,10 +285,11 @@
             ]
             corr = jnp.dot(main, jnp.concatenate(pairs, axis=0), preferred_element_type=jnp.float32)
             scale = inverse[j, s]
-            results.append(totals[j] + (corr.reshape(SLOTS, PH, LANES) * scale[None]) * gain[:, None, :])
+            corr = corr.reshape(SLOTS, PH, LANES)
+            results.append(tuple(totals[j][k] + (corr[k] * scale) * gain[k] for k in range(SLOTS)))
         return tuple(results)
 
-    totals = tuple(jnp.zeros((SLOTS, PH, LANES), jnp.float32) for _ in range(tiles))
+    totals = tuple(tuple(jnp.zeros((PH, LANES), jnp.float32) for _ in range(SLOTS)) for _ in range(tiles))
     gain_copy.wait()
 
     def part(c, totals):
@@ -266,17 +300,12 @@
     totals = lax.fori_loop(0, stations // chunk, part, totals)
 
     lane = lane_ids((KB, LANES))
-    source = lax.broadcasted_iota(jnp.int32, (KB, LANES), 0) * width + lane // PH
+    source = lane % PH * width + lane // PH
     for j in range(tiles):
         for b in range(NB):
-            tile = swap_groups([totals[j][b * KB + k] for k in range(KB)], width)
-            for at in range(per_tile):
-                value = None
-                for p in range(PH):
-                    one = jnp.broadcast_to(tile[at][p : p + 1, :], (KB, LANES))
-                    one = jnp.take_along_axis(one, source, axis=1)
-                    value = one if value is None else jnp.where(lane % PH == p, one, value)
-                out[j * per_tile + at, b] = value
+            tile = jnp.swapaxes(jnp.stack(totals[j][b * KB : (b + 1) * KB]), 0, 1)
+            for at, value in enumerate(swap_groups([tile[p] for p in range(PH)], width)):
+                out[j * per_tile + at, b] = jnp.take_along_axis(value, source, axis=1)
 
 
 def correlate(moved, following, shifts, coef):
@@ -296,7 +325,7 @@
         scratch_shapes=[
             pltpu.VMEM(shifts.shape, jnp.bfloat16),
             pltpu.VMEM(coef.shape, jnp.float32),
-            pltpu.VMEM((stations, following.shape[1]), jnp.bfloat16),
+            pltpu.VMEM(following.shape, jnp.bfloat16),
             pltpu.VMEM((tiles + 1, stations, PH, LANES), jnp.float32),
             pltpu.VMEM((tiles, stations, PH, LANES), jnp.float32),
             pltpu.SemaphoreType.DMA((stations // chunk,)),
@@ -314,8 +343,8 @@
     block_len = records.shape[1]
     stations = library.shape[1]
     moved = lax.all_to_all(records.reshape(owners, stations, block_len), "tm", split_axis=0, concat_axis=0)
-    shifts, coef = prepare(template_ids, library, channel_mask, station_group)
-    partial_sum = correlate(moved, following, shifts, coef)
+    shifts, coef, after = prepare(template_ids, library, channel_mask, station_group, following)
+    partial_sum = correlate(moved, after, shifts, coef)
     parts = lax.all_to_all(
         partial_sum.reshape(owners * NB, KB, block_len), ("tm", "sta"), split_axis=0, concat_axis=0
     )

time: 37.8 us -> 36.4 us (0.963)
  local copies, waits for them, and re-layouts: 0.68 us -> 0 us
  waiting for transfers between devices: 1.19 us -> 1.86 us
  Pallas kernels: 16 us -> 15.4 us
  blocking collectives: 11.6 us -> 11 us
    unnamed x2 -> x0, local copies, waits for them, and re-layouts: 0.68 us -> none
    all_to_all x1, blocking collectives: 11.6 us -> 11 us  [shards(): lax.all_to_all(partial_sum.reshape(owners * NB, KB, block_len), ('tm', 's...]
    all_to_all x1, waiting for transfers between devices: 1.19 us -> 1.86 us  [shards(): lax.all_to_all(records.reshape(owners, stations, block_len), 'tm', split_...]
    pallas_call x1, Pallas kernels: 8.94 us -> 8.31 us  [correlate(): pl.pallas_call(functools.partial(correlate_kernel, chunk), out_shape=jax....]
  transfers between devices with their start and end apart: 1 -> 1, of which waited for: 1 -> 1; matrix products, arithmetic and copies ran while one was open for 0% -> 0% of each run, Pallas kernels for 19% -> 20%
where the time goes in v4:
time: 36.4 us; the launch traced here: 36.1 us
  Pallas kernels  15.4 us (42%)
  blocking collectives  11 us (30%)
  starting transfers between devices  7.28 us (20%)
  waiting for transfers between devices  1.86 us (5%)
  other arithmetic  0.61 us (2%)
    all_to_all x1, blocking collectives, shards(): lax.all_to_all(partial_sum.reshape(owners * NB, KB, block_len), ('tm', 's...  11 us
    pallas_call x1, Pallas kernels, correlate(): pl.pallas_call(functools.partial(correlate_kernel, chunk), out_shape=jax....  8.31 us
    all_to_all x1, starting transfers between devices, shards(): lax.all_to_all(records.reshape(owners, stations, block_len), 'tm', split_...  7.28 us
    pallas_call x1, Pallas kernels, prepare(): pl.pallas_call(functools.partial(prepare_kernel, chunk), out_shape=(pltpu...  7.05 us
    all_to_all x1, waiting for transfers between devices, shards(): lax.all_to_all(records.reshape(owners, stations, block_len), 'tm', split_...  1.86 us
  transfers between devices with their start and end apart: 1, of which 1 were waited for; matrix products, arithmetic and copies ran while one was open for 0% of the time, Pallas kernels for 20%

profile of v4, /device:TPU:0, one launch (start us, length us, event | category | flops | bytes accessed | tf_op | source)
XLA Modules:
  0.0 36.1 jit_solution(17591089794372287121)
XLA Ops:
  0.0 7.3 %all-to-all-start = ((bf16[8,128,128]{2,1,0:T(8,128)(2,1)}), bf16[8,128,128]{2,1,0:T(8,128)(2,1)S(1)}, u32[]{:S(2)}, u32[]{:S(2)}) async-start(bf16[8,128,128]{2,1,0:T(8,128)(2,1)} %bitcast.5), calls=%async_computation | async-start | bytes 524288 | tf_op jit(solution)/shard_map/all_to_all | solution.py:345
  7.3 7.1 %prepare.1 = (bf16[128,128,256]{2,1,0:T(8,128)(2,1)}, f32[128,16,128]{2,1,0:T(8,128)}, bf16[128,256]{1,0:T(8,128)(2,1)}) custom-call(s32[2,8]{1,0:T(2,128)} %ids.1, bf16[32,128,256]{2,1,0:T(8,128)(2,1)} %library.1, s32[32,2048]{1,0:T(8,128)} %mask.1, s32[1,2048]{1,0:T(1,128)} %bitcast.6, bf16[1024,255]{1,0:T(8,128)(2,1)} %following.1), custom_call_target="tpu_custom_call" | custom-call | flops 10000000 | bytes 20000000 | tf_op jit(solution)/shard_map/prepare/pallas_call | solution.py:167
  14.3 1.9 %all-to-all-done.moved = bf16[8,128,128]{2,1,0:T(8,128)(2,1)S(1)} async-done(((bf16[8,128,128]{2,1,0:T(8,128)(2,1)}), bf16[8,128,128]{2,1,0:T(8,128)(2,1)S(1)}, u32[]{:S(2)}, u32[]{:S(2)}) %all-to-all-start) | async-done | bytes 262176 | tf_op jit(solution)/shard_map/all_to_all | solution.py:345
  16.2 8.3 %correlate.1 = f32[8,2,8,128]{3,2,1,0:T(8,128)S(1)} custom-call(bf16[8,128,128]{2,1,0:T(8,128)(2,1)S(1)} %all-to-all-done.moved, bf16[128,256]{1,0:T(8,128)(2,1)} %get-tuple-element.8.following, bf16[128,128,256]{2,1,0:T(8,128)(2,1)} %get-tuple-element.9.shifts, f32[128,16,128]{2,1,0:T(8,128)} %get-tuple-element.10.coef), custom_call_target="tpu_custom_call" | custom-call | flops 1200000000 | bytes 10000000 | tf_op jit(solution)/shard_map/correlate/pallas_call | solution.py:315
  24.5 11.0 %all_to_all.10 = f32[16,8,128]{2,1,0:T(8,128)S(1)} all-to-all(f32[16,8,128]{2,1,0:T(8,128)S(1)} %bitcast.4), channel_id=1, replica_groups=mesh['days'=2,'tm'=8,'sta'=2] {'tm','sta'}, dimensions={0} | all-to-all | bytes 131072 | tf_op jit(solution)/shard_map/all_to_all | solution.py:348
  35.5 0.6 %reduce_sum.9 = f32[8,128]{1,0:T(8,128)} reduce(f32[16,8,128]{2,1,0:T(8,128)S(1)} %all_to_all.10, f32[]{:T(128)} %constant.0.clone.1), dimensions={0}, to_apply=%region_0.0 | reduce | flops 15360 | bytes 69636 | tf_op jit(solution)/shard_map/reduce_sum | solution.py:351
Async XLA Ops:
  0.0 16.2 %all-to-all-start = ((bf16[8,128,128]{2,1,0:T(8,128)(2,1)}), bf16[8,128,128]{2,1,0:T(8,128)(2,1)S(1)}, u32[]{:S(2)}, u32[]{:S(2)}) async-start(bf16[8,128,128]{2,1,0:T(8,128)(2,1)} %bitcast.5), calls=%async_computation | async-start | bytes 524288 | tf_op jit(solution)/shard_map/all_to_all | solution.py:345

commit v5 on v4

--- a/solution.py
+++ b/solution.py
@@ -19,6 +19,9 @@
 PIECES = LANES // TAPS
 VMEM = 24 << 20
 CHUNK = 64
+UNROLL = 32
+TURNS = LANES // PH
+MADE = (8, 12, 4)
 
 epsilon = 1e-06
 
@@ -51,7 +54,6 @@
 
 
 def prepare_kernel(
-    chunk,
     ids,
     library,
     mask,
@@ -60,27 +62,28 @@
     shifts,
     coef,
     after,
+    edges,
     picked,
     wide,
     rows,
     made,
     gains,
     own_tail,
-    tail,
+    edge,
     row_sem,
     in_sem,
     tail_sem,
     out_sem,
     gain_sem,
-    after_sem,
+    edge_sem,
 ):
     stations = library.shape[1]
     total = mask.shape[1]
     position = lax.axis_index("tm")
     for k in range(SLOTS):
+        pltpu.make_async_copy(library.at[ids[k // KB, k % KB]], picked.at[k], in_sem).start()
+    for k in range(SLOTS):
         pltpu.make_async_copy(mask.at[pl.ds(ids[k // KB, k % KB], 1)], rows.at[pl.ds(k, 1)], row_sem).start()
-    for k in range(SLOTS):
-        pltpu.make_async_copy(library.at[ids[k // KB, k % KB]], picked.at[k], in_sem).start()
     tail_in = pltpu.make_async_copy(following.at[pl.ds(position * stations, stations)], own_tail, tail_sem)
     tail_in.start()
 
@@ -117,59 +120,61 @@
     gains_out = pltpu.make_async_copy(gains, coef, gain_sem)
     gains_out.start()
     tail_in.wait()
-    tail[...] = jnp.concatenate([own_tail[...], jnp.zeros((stations, 1), jnp.bfloat16)], axis=1)
-    tail_out = pltpu.make_async_copy(tail, after, after_sem)
-    tail_out.start()
+    after[...] = jnp.concatenate([own_tail[...], jnp.zeros((stations, 1), jnp.bfloat16)], axis=1)
 
     lane = lane_ids((PH, LANES))
     row = lax.broadcasted_iota(jnp.int32, (PH, LANES), 0)
-    inside = lane >= row
-
-    def station(s):
-        for pair in range(SLOTS // 2):
+
+    def part(c, carry):
+        rest = [jnp.zeros((PH, LANES), jnp.float32) for _ in range(SLOTS)]
+        for i in range(TURNS):
+            s = c * TURNS + i
+            inside = lane >= row + PH * i
+            wrapped = lane < PH * i
             halves = []
-            for k in (2 * pair, 2 * pair + 1):
+            for k in range(SLOTS):
                 template = wide[k, pl.ds(s, 1), :]
                 turned = [
                     pltpu.roll(
-                        jnp.broadcast_to(template[:, h * LANES : (h + 1) * LANES], (PH, LANES)), 0, 1, stride=1, stride_axis=0
+                        jnp.broadcast_to(template[:, h * LANES : (h + 1) * LANES], (PH, LANES)),
+                        PH * i,
+                        1,
+                        stride=1,
+                        stride_axis=0,
                     )
                     for h in range(W // LANES)
                 ]
-                halves.append(
-                    jnp.concatenate(
-                        [jnp.where(inside, turned[h], turned[h - 1]) for h in range(W // LANES)], axis=1
-                    )
-                )
-            made[s, 2 * PH * pair : 2 * PH * (pair + 1), :] = jnp.concatenate(halves, axis=0).astype(jnp.bfloat16)
-
-    def part(c, carry):
-        def step(i, inner):
-            station(c * chunk + i)
-            return inner
-
-        lax.fori_loop(0, chunk, step, 0, unroll=True)
-        span = pl.ds(c * chunk, chunk)
+                ahead = jnp.where(wrapped, turned[-1], 0.0)
+                rest[k] = jnp.where(inside, rest[k], jnp.where(wrapped, rest[k], turned[-1]))
+                columns = [jnp.where(inside, turned[h], turned[h - 1] if h else ahead) for h in range(W // LANES)]
+                halves.append(jnp.concatenate(columns, axis=1))
+            for pair in range(SLOTS // 2):
+                value = jnp.concatenate(halves[2 * pair : 2 * pair + 2], axis=0).astype(jnp.bfloat16)
+                made[s, 2 * PH * pair : 2 * PH * (pair + 1), :] = value
+        edge[c] = jnp.concatenate(rest, axis=0).astype(jnp.bfloat16)
+        span = pl.ds(c * TURNS, TURNS)
         pltpu.make_async_copy(made.at[span], shifts.at[span], out_sem).start()
         return carry
 
-    lax.fori_loop(0, stations // chunk, part, 0)
+    lax.fori_loop(0, stations // TURNS, part, 0)
+    edge_out = pltpu.make_async_copy(edge, edges, edge_sem)
+    edge_out.start()
     gains_out.wait()
-    tail_out.wait()
     pltpu.make_async_copy(made, shifts, out_sem).wait()
+    edge_out.wait()
 
 
 def prepare(template_ids, library, channel_mask, station_group, following):
     stations = library.shape[1]
     total = channel_mask.shape[1]
-    chunk = min(16, stations)
     inputs = template_ids, library, channel_mask, station_group.reshape(1, total), following
     return pl.pallas_call(
-        functools.partial(prepare_kernel, chunk),
+        prepare_kernel,
         out_shape=(
             pltpu.HBM((stations, SLOTS * PH, W), jnp.bfloat16),
             pltpu.HBM((stations, SLOTS, LANES), jnp.float32),
-            pltpu.HBM((stations, W), jnp.bfloat16),
+            pltpu.VMEM((stations, W), jnp.bfloat16),
+            pltpu.HBM((stations // TURNS, SLOTS * PH, LANES), jnp.bfloat16),
         ),
         in_specs=[
             pl.BlockSpec(memory_space=pltpu.SMEM),
@@ -178,7 +183,7 @@
             pl.BlockSpec(memory_space=pltpu.VMEM),
             pl.BlockSpec(memory_space=pl.ANY),
         ],
-        out_specs=[pl.BlockSpec(memory_space=pl.ANY)] * 3,
+        out_specs=[pl.BlockSpec(memory_space=space) for space in (pl.ANY, pl.ANY, pltpu.VMEM, pl.ANY)],
         scratch_shapes=[
             pltpu.VMEM((SLOTS, stations, W), jnp.bfloat16),
             pltpu.VMEM((SLOTS, stations, W), jnp.float32),
@@ -186,7 +191,7 @@
             pltpu.VMEM((stations, SLOTS * PH, W), jnp.bfloat16),
             pltpu.VMEM((stations, SLOTS, LANES), jnp.float32),
             pltpu.VMEM((stations, following.shape[1]), jnp.bfloat16),
-            pltpu.VMEM((stations, W), jnp.bfloat16),
+            pltpu.VMEM((stations // TURNS, SLOTS * PH, LANES), jnp.bfloat16),
         ]
         + [pltpu.SemaphoreType.DMA] * 6,
         compiler_params=pltpu.CompilerParams(vmem_limit_bytes=VMEM),
@@ -195,23 +200,21 @@
     )(*(pltpu.with_memory_space_constraint(v, pltpu.HBM) for v in inputs))
 
 
-def correlate_kernel(chunk, moved, following, shifts, coef, out, held, gains, tail, phases, inverse, held_sems, gain_sem, tail_sem):
+def correlate_kernel(chunk, moved, following, shifts, coef, edges, out, held, gains, edge, phases, inverse, windows, held_sems, gain_sem, edge_sem):
     owners, stations, block_len = moved.shape
     width = block_len // PH
     tiles = owners * block_len // (LANES * PH)
     per_tile = LANES // width
 
-    tail_copy = pltpu.make_async_copy(following, tail, tail_sem)
-    tail_copy.start()
-    held_copies = [
-        pltpu.make_async_copy(shifts.at[pl.ds(c, chunk)], held.at[pl.ds(c, chunk)], held_sems.at[c // chunk])
-        for c in range(0, stations, chunk)
-    ]
-    held_copies[0].start()
+    def held_copy(c):
+        span = pl.ds(c * chunk, chunk)
+        return pltpu.make_async_copy(shifts.at[span], held.at[span], held_sems.at[c])
+
+    held_copy(0).start()
     gain_copy = pltpu.make_async_copy(coef, gains, gain_sem)
     gain_copy.start()
-    for copy in held_copies[1:]:
-        copy.start()
+    edge_copy = pltpu.make_async_copy(edges, edge, edge_sem)
+    edge_copy.start()
 
     time = lax.broadcasted_iota(jnp.int32, (W, W), 0)
     place = lax.broadcasted_iota(jnp.int32, (W, W), 1)
@@ -240,8 +243,7 @@
     for j in range(tiles):
         pieces = [split(r) for r in rows[j * PIECES : (j + 1) * PIECES]]
         keep(phases, j, [v for h in range(PH // PIECES) for v in swap_groups([p[h] for p in pieces], TAPS)])
-    tail_copy.wait()
-    rows.append(tail[...])
+    rows.append(following[...])
     last = split(rows[-1])
     keep(
         phases,
@@ -251,6 +253,21 @@
             for p in range(PH)
         ],
     )
+
+    ahead = time - place % LANES - place // LANES
+    for parity in range(2):
+        for n in range(len(MADE) + 1):
+            if n:
+                matrix = ahead == 2 * MADE[n - 1] - parity
+            else:
+                matrix = jnp.logical_and(ahead == TAPS - parity, place // LANES == parity)
+            matrix = matrix.astype(jnp.float32).astype(jnp.bfloat16)
+            for j in range(tiles):
+                value = jnp.concatenate([phases[j], phases[j + 1]], axis=2).reshape(stations // 2, 2, PH, W)[:, parity]
+                value = value.reshape(stations // 2 * PH, W).astype(jnp.bfloat16)
+                value = jnp.dot(value, matrix, preferred_element_type=jnp.float32)
+                value = [value[:, h * LANES : (h + 1) * LANES].reshape(stations // 2, PH, LANES) for h in range(2)]
+                windows[n, j, parity] = jnp.concatenate(value, axis=1).astype(jnp.bfloat16)
 
     squared = [squares(r) for r in rows]
     for j in range(tiles):
@@ -265,37 +282,57 @@
             pieces.append([energy[:, h * LANES : (h + 1) * LANES] for h in range(W // LANES)])
         keep(inverse, j, [v for h in range(PH // PIECES) for v in swap_groups([p[h] for p in pieces], TAPS)])
 
-    row = lax.broadcasted_iota(jnp.int32, (2 * PH, LANES), 0) % PH
-    inside = (lane_ids((2 * PH, LANES)) >= row).astype(jnp.float32).astype(jnp.bfloat16)
-
-    def station(s, totals):
-        templates = held[s]
-        head = templates[:, :LANES].reshape(SLOTS // 2, 2 * PH, LANES)
-        kept = head * inside[None]
-        rest = (head - kept).reshape(SLOTS * PH, LANES)[:, : 2 * PH]
-        main = jnp.concatenate([kept.reshape(SLOTS * PH, LANES), templates[:, LANES:], rest], axis=1)
-        gain = [jnp.broadcast_to(gains[s, pl.ds(k, 1), :], (PH, LANES)) for k in range(SLOTS)]
-        own = [phases[j, s] for j in range(tiles + 1)]
+    nothing = jnp.zeros((2 * PH, LANES), jnp.bfloat16)
+
+    def window(s, turn, j):
+        own, after = phases[j, s], phases[j + 1, s]
+        pairs = []
+        for i in range(TAPS // 2):
+            first = (2 * i - turn) % TAPS
+            if (first + 1) // 2 in MADE:
+                pairs.append(windows[1 + MADE.index((first + 1) // 2), j, turn % 2, s // 2])
+            else:
+                pair = [shifted(own, after, by % TAPS) for by in (first, first + 1)]
+                pairs.append(jnp.concatenate(pair, axis=0).astype(jnp.bfloat16))
+        return jnp.concatenate(pairs, axis=0)
+
+    def two_stations(group, turn, totals):
+        s = group * TURNS + turn
         results = []
         for j in range(tiles):
-            window = [shifted(own[j], own[j + 1], by) for by in range(TAPS + 1)]
-            window.append(jnp.zeros_like(own[j]))
-            pairs = [
-                jnp.concatenate(window[2 * i : 2 * i + 2], axis=0).astype(jnp.bfloat16) for i in range(TAPS // 2 + 1)
+            ends = [
+                jnp.concatenate([windows[0, j, e, s // 2] if i == turn // 2 else nothing for i in range(LANES // (2 * PH))], axis=0)
+                for e in range(2)
             ]
-            corr = jnp.dot(main, jnp.concatenate(pairs, axis=0), preferred_element_type=jnp.float32)
-            scale = inverse[j, s]
-            corr = corr.reshape(SLOTS, PH, LANES)
-            results.append(tuple(totals[j][k] + (corr[k] * scale) * gain[k] for k in range(SLOTS)))
+            ends = jnp.dot(edge[group], jnp.concatenate(ends, axis=1), preferred_element_type=jnp.float32)
+            total = totals[j]
+            for e in range(2):
+                corr = jnp.dot(held[s + e], window(s + e, turn + e, j), preferred_element_type=jnp.float32)
+                corr = (corr + ends[:, e * LANES : (e + 1) * LANES]).reshape(SLOTS, PH, LANES)
+                scale = inverse[j, s + e]
+                gain = [jnp.broadcast_to(gains[s + e, pl.ds(k, 1), :], (PH, LANES)) for k in range(SLOTS)]
+                total = tuple(total[k] + (corr[k] * scale) * gain[k] for k in range(SLOTS))
+            results.append(total)
         return tuple(results)
 
     totals = tuple(tuple(jnp.zeros((PH, LANES), jnp.float32) for _ in range(SLOTS)) for _ in range(tiles))
     gain_copy.wait()
+    edge_copy.wait()
 
     def part(c, totals):
-        span = pl.ds(c * chunk, chunk)
-        pltpu.make_async_copy(shifts.at[span], held.at[span], held_sems.at[c]).wait()
-        return lax.fori_loop(0, chunk, lambda i, totals: station(c * chunk + i, totals), totals, unroll=True)
+        held_copy(c).wait()
+
+        @pl.when(c + 1 < stations // chunk)
+        def _():
+            held_copy(c + 1).start()
+
+        def some(i, totals):
+            for g in range(UNROLL // TURNS):
+                for turn in range(0, TURNS, 2):
+                    totals = two_stations(c * (chunk // TURNS) + i * (UNROLL // TURNS) + g, turn, totals)
+            return totals
+
+        return lax.fori_loop(0, chunk // UNROLL, some, totals)
 
     totals = lax.fori_loop(0, stations // chunk, part, totals)
 
@@ -308,7 +345,7 @@
                 out[j * per_tile + at, b] = jnp.take_along_axis(value, source, axis=1)
 
 
-def correlate(moved, following, shifts, coef):
+def correlate(moved, following, shifts, coef, edges):
     owners, stations, block_len = moved.shape
     tiles = owners * block_len // (LANES * PH)
     chunk = math.gcd(stations, CHUNK)
@@ -317,6 +354,7 @@
         out_shape=jax.ShapeDtypeStruct((owners, NB, KB, LANES), jnp.float32),
         in_specs=[
             pl.BlockSpec(memory_space=pltpu.VMEM),
+            pl.BlockSpec(memory_space=pltpu.VMEM),
             pl.BlockSpec(memory_space=pl.ANY),
             pl.BlockSpec(memory_space=pl.ANY),
             pl.BlockSpec(memory_space=pl.ANY),
@@ -325,9 +363,10 @@
         scratch_shapes=[
             pltpu.VMEM(shifts.shape, jnp.bfloat16),
             pltpu.VMEM(coef.shape, jnp.float32),
-            pltpu.VMEM(following.shape, jnp.bfloat16),
+            pltpu.VMEM(edges.shape, jnp.bfloat16),
             pltpu.VMEM((tiles + 1, stations, PH, LANES), jnp.float32),
             pltpu.VMEM((tiles, stations, PH, LANES), jnp.float32),
+            pltpu.VMEM((len(MADE) + 1, tiles, 2, stations // 2, 2 * PH, LANES), jnp.bfloat16),
             pltpu.SemaphoreType.DMA((stations // chunk,)),
             pltpu.SemaphoreType.DMA,
             pltpu.SemaphoreType.DMA,
@@ -335,7 +374,11 @@
         compiler_params=pltpu.CompilerParams(vmem_limit_bytes=VMEM),
         cost_estimate=pl.CostEstimate(flops=1_200_000_000, bytes_accessed=10_000_000, transcendentals=0),
         name="correlate",
-    )(moved, *(pltpu.with_memory_space_constraint(v, pltpu.HBM) for v in (following, shifts, coef)))
+    )(
+        moved,
+        pltpu.with_memory_space_constraint(following, pltpu.VMEM),
+        *(pltpu.with_memory_space_constraint(v, pltpu.HBM) for v in (shifts, coef, edges)),
+    )
 
 
 def shards(records, following, library, template_ids, channel_mask, station_group):
@@ -343,8 +386,8 @@
     block_len = records.shape[1]
     stations = library.shape[1]
     moved = lax.all_to_all(records.reshape(owners, stations, block_len), "tm", split_axis=0, concat_axis=0)
-    shifts, coef, after = prepare(template_ids, library, channel_mask, station_group, following)
-    partial_sum = correlate(moved, after, shifts, coef)
+    shifts, coef, after, edges = prepare(template_ids, library, channel_mask, station_group, following)
+    partial_sum = correlate(moved, after, shifts, coef, edges)
     parts = lax.all_to_all(
         partial_sum.reshape(owners * NB, KB, block_len), ("tm", "sta"), split_axis=0, concat_axis=0
     )

time: 36.4 us -> 36.7 us (level)
  no operation moved by 1% of the time
where the time goes in v5:
time: 36.7 us; the launch traced here: 36.2 us
  Pallas kernels  15.5 us (42%)
  blocking collectives  11.2 us (31%)
  starting transfers between devices  7.28 us (20%)
  waiting for transfers between devices  1.56 us (4%)
  other arithmetic  0.61 us (2%)
    all_to_all x1, blocking collectives, shards(): lax.all_to_all(partial_sum.reshape(owners * NB, KB, block_len), ('tm', 's...  11.2 us
    pallas_call x1, Pallas kernels, correlate(): pl.pallas_call(functools.partial(correlate_kernel, chunk), out_shape=jax....  8.17 us
    pallas_call x1, Pallas kernels, prepare(): pl.pallas_call(prepare_kernel, out_shape=(pltpu.HBM((stations, SLOTS * PH...  7.35 us
    all_to_all x1, starting transfers between devices, shards(): lax.all_to_all(records.reshape(owners, stations, block_len), 'tm', split_...  7.28 us
    all_to_all x1, waiting for transfers between devices, shards(): lax.all_to_all(records.reshape(owners, stations, block_len), 'tm', split_...  1.56 us
  transfers between devices with their start and end apart: 1, of which 1 were waited for; matrix products, arithmetic and copies ran while one was open for 0% of the time, Pallas kernels for 20%

profile of v5, /device:TPU:0, one launch (start us, length us, event | category | flops | bytes accessed | tf_op | source)
XLA Modules:
  0.0 36.2 jit_solution(5169313915417682778)
XLA Ops:
  0.0 7.3 %all-to-all-start = ((bf16[8,128,128]{2,1,0:T(8,128)(2,1)}), bf16[8,128,128]{2,1,0:T(8,128)(2,1)S(1)}, u32[]{:S(2)}, u32[]{:S(2)}) async-start(bf16[8,128,128]{2,1,0:T(8,128)(2,1)} %bitcast.5), calls=%async_computation | async-start | bytes 524288 | tf_op jit(solution)/shard_map/all_to_all | solution.py:388
  7.3 7.3 %prepare.1 = (bf16[128,128,256]{2,1,0:T(8,128)(2,1)}, f32[128,16,128]{2,1,0:T(8,128)}, bf16[128,256]{1,0:T(8,128)(2,1)S(1)}, bf16[8,128,128]{2,1,0:T(8,128)(2,1)}) custom-call(s32[2,8]{1,0:T(2,128)} %ids.1, bf16[32,128,256]{2,1,0:T(8,128)(2,1)} %library.1, s32[32,2048]{1,0:T(8,128)} %mask.1, s32[1,2048]{1,0:T(1,128)} %bitcast.6, bf16[1024,255]{1,0:T(8,128)(2,1)} %following.1), custom_call_target="tpu_custom_call" | custom-call | flops 10000000 | bytes 20000000 | tf_op jit(solution)/shard_map/prepare/pallas_call | solution.py:171
  14.6 1.6 %all-to-all-done.moved = bf16[8,128,128]{2,1,0:T(8,128)(2,1)S(1)} async-done(((bf16[8,128,128]{2,1,0:T(8,128)(2,1)}), bf16[8,128,128]{2,1,0:T(8,128)(2,1)S(1)}, u32[]{:S(2)}, u32[]{:S(2)}) %all-to-all-start) | async-done | bytes 262176 | tf_op jit(solution)/shard_map/all_to_all | solution.py:388
  16.2 8.2 %correlate.1 = f32[8,2,8,128]{3,2,1,0:T(8,128)S(1)} custom-call(bf16[8,128,128]{2,1,0:T(8,128)(2,1)S(1)} %all-to-all-done.moved, bf16[128,256]{1,0:T(8,128)(2,1)S(1)} %get-tuple-element.9.following, bf16[128,128,256]{2,1,0:T(8,128)(2,1)} %get-tuple-element.10.shifts, f32[128,16,128]{2,1,0:T(8,128)} %get-tuple-element.11.coef, ...), custom_call_target="tpu_custom_call" | custom-call | flops 1200000000 | bytes 10000000 | tf_op jit(solution)/shard_map/correlate/pallas_call | solution.py:352
  24.4 11.2 %all_to_all.10 = f32[16,8,128]{2,1,0:T(8,128)S(1)} all-to-all(f32[16,8,128]{2,1,0:T(8,128)S(1)} %bitcast.4), channel_id=1, replica_groups=mesh['days'=2,'tm'=8,'sta'=2] {'tm','sta'}, dimensions={0} | all-to-all | bytes 131072 | tf_op jit(solution)/shard_map/all_to_all | solution.py:391
  35.6 0.6 %reduce_sum.9 = f32[8,128]{1,0:T(8,128)} reduce(f32[16,8,128]{2,1,0:T(8,128)S(1)} %all_to_all.10, f32[]{:T(128)} %constant.0.clone.1), dimensions={0}, to_apply=%region_0.0 | reduce | flops 15360 | bytes 69636 | tf_op jit(solution)/shard_map/reduce_sum | solution.py:394
Async XLA Ops:
  0.0 16.2 %all-to-all-start = ((bf16[8,128,128]{2,1,0:T(8,128)(2,1)}), bf16[8,128,128]{2,1,0:T(8,128)(2,1)S(1)}, u32[]{:S(2)}, u32[]{:S(2)}) async-start(bf16[8,128,128]{2,1,0:T(8,128)(2,1)} %bitcast.5), calls=%async_computation | async-start | bytes 524288 | tf_op jit(solution)/shard_map/all_to_all | solution.py:388

commit v6 on v5

--- a/solution.py
+++ b/solution.py
@@ -19,9 +19,10 @@
 PIECES = LANES // TAPS
 VMEM = 24 << 20
 CHUNK = 64
-UNROLL = 32
+AHEAD = 1
+UNROLL = 64
 TURNS = LANES // PH
-MADE = (8, 12, 4)
+MADE = (8, 4)
 
 epsilon = 1e-06
 
@@ -69,12 +70,14 @@
     made,
     gains,
     own_tail,
+    tail,
     edge,
     row_sem,
     in_sem,
     tail_sem,
     out_sem,
     gain_sem,
+    after_sem,
     edge_sem,
 ):
     stations = library.shape[1]
@@ -87,40 +90,14 @@
     tail_in = pltpu.make_async_copy(following.at[pl.ds(position * stations, stations)], own_tail, tail_sem)
     tail_in.start()
 
-    members = lax.broadcasted_iota(jnp.int32, (G, total), 0) == group[...]
-    members = members.astype(jnp.float32).astype(jnp.bfloat16)
-    pltpu.make_async_copy(mask.at[pl.ds(0, SLOTS)], rows, row_sem).wait()
-    counts = lax.dot_general(
-        rows[...].astype(jnp.float32).astype(jnp.bfloat16),
-        members,
-        (((1,), (1,)), ((), ())),
-        preferred_element_type=jnp.float32,
-    )
-    first = lax.axis_index("sta") * (stations * lax.axis_size("tm")) + position * stations
-    block = pl.multiple_of(first // LANES * LANES, LANES)
-    own_group = jnp.broadcast_to(group[:, pl.ds(block, LANES)], (G, LANES))
-    own_mask = rows[:, pl.ds(block, LANES)].astype(jnp.float32)
-    own = (lax.broadcasted_iota(jnp.int32, (G, LANES), 0) == own_group).astype(jnp.float32)
-    per_station = jnp.dot(counts, own, preferred_element_type=jnp.float32, precision=lax.Precision.HIGHEST)
-    scaled = own_mask / jnp.sqrt(jnp.float32(W * G) * jnp.maximum(per_station, 1.0))
-    if stations % LANES:
-        scaled = pltpu.roll(scaled, LANES - (first - block), 1)
-    scaled = jnp.concatenate([scaled, jnp.zeros((LANES - SLOTS, LANES), jnp.float32)], axis=0).T
-
     for k in range(SLOTS):
         pltpu.make_async_copy(library.at[0], picked.at[k], in_sem).wait()
-    columns = []
     for k in range(SLOTS):
-        values = picked[k].astype(jnp.float32)
-        wide[k] = values
-        tmean = jnp.sum(values * values, axis=1, keepdims=True) / W
-        value = scaled[:stations, k : k + 1] / jnp.sqrt(tmean + epsilon)
-        columns.append(jnp.broadcast_to(value, (stations, LANES)))
-    gains[...] = jnp.swapaxes(jnp.stack(columns), 0, 1)
-    gains_out = pltpu.make_async_copy(gains, coef, gain_sem)
-    gains_out.start()
+        wide[k] = picked[k].astype(jnp.float32)
     tail_in.wait()
-    after[...] = jnp.concatenate([own_tail[...], jnp.zeros((stations, 1), jnp.bfloat16)], axis=1)
+    tail[...] = jnp.concatenate([own_tail[...], jnp.zeros((stations, 1), jnp.bfloat16)], axis=1)
+    tail_out = pltpu.make_async_copy(tail, after, after_sem)
+    tail_out.start()
 
     lane = lane_ids((PH, LANES))
     row = lax.broadcasted_iota(jnp.int32, (PH, LANES), 0)
@@ -159,7 +136,42 @@
     lax.fori_loop(0, stations // TURNS, part, 0)
     edge_out = pltpu.make_async_copy(edge, edges, edge_sem)
     edge_out.start()
+
+    members = lax.broadcasted_iota(jnp.int32, (G, total), 0) == group[...]
+    members = members.astype(jnp.float32).astype(jnp.bfloat16)
+    pltpu.make_async_copy(mask.at[pl.ds(0, SLOTS)], rows, row_sem).wait()
+    counts = lax.dot_general(
+        rows[...].astype(jnp.float32).astype(jnp.bfloat16),
+        members,
+        (((1,), (1,)), ((), ())),
+        preferred_element_type=jnp.float32,
+    )
+    first = lax.axis_index("sta") * (stations * lax.axis_size("tm")) + position * stations
+    block = pl.multiple_of(first // LANES * LANES, LANES)
+    own_group = jnp.broadcast_to(group[:, pl.ds(block, LANES)], (G, LANES))
+    own_mask = rows[:, pl.ds(block, LANES)].astype(jnp.float32)
+    own = (lax.broadcasted_iota(jnp.int32, (G, LANES), 0) == own_group).astype(jnp.float32)
+    per_station = jnp.dot(counts, own, preferred_element_type=jnp.float32, precision=lax.Precision.HIGHEST)
+    scaled = own_mask / jnp.sqrt(jnp.float32(W * G) * jnp.maximum(per_station, 1.0))
+    if stations % LANES:
+        scaled = pltpu.roll(scaled, LANES - (first - block), 1)
+    sums = jnp.zeros((stations, LANES), jnp.float32)
+    for k in range(SLOTS):
+        values = jnp.square(wide[k])
+        values = sum(values[:, h * LANES : (h + 1) * LANES] for h in range(W // LANES))
+        high = values.astype(jnp.bfloat16)
+        low = (values - high.astype(jnp.float32)).astype(jnp.bfloat16)
+        column = (lane_ids((LANES, LANES)) == k).astype(jnp.float32).astype(jnp.bfloat16)
+        sums = sums + jnp.dot(high, column, preferred_element_type=jnp.float32)
+        sums = sums + jnp.dot(low, column, preferred_element_type=jnp.float32)
+    if stations < LANES:
+        sums = jnp.concatenate([sums, jnp.zeros((LANES - stations, LANES), jnp.float32)], axis=0)
+    gains[...] = scaled / jnp.sqrt(sums.T[:SLOTS] / W + epsilon)
+    gains_out = pltpu.make_async_copy(gains, coef, gain_sem)
+    gains_out.start()
+
     gains_out.wait()
+    tail_out.wait()
     pltpu.make_async_copy(made, shifts, out_sem).wait()
     edge_out.wait()
 
@@ -172,8 +184,8 @@
         prepare_kernel,
         out_shape=(
             pltpu.HBM((stations, SLOTS * PH, W), jnp.bfloat16),
-            pltpu.HBM((stations, SLOTS, LANES), jnp.float32),
-            pltpu.VMEM((stations, W), jnp.bfloat16),
+            pltpu.HBM((SLOTS, LANES), jnp.float32),
+            pltpu.HBM((stations, W), jnp.bfloat16),
             pltpu.HBM((stations // TURNS, SLOTS * PH, LANES), jnp.bfloat16),
         ),
         in_specs=[
@@ -183,38 +195,42 @@
             pl.BlockSpec(memory_space=pltpu.VMEM),
             pl.BlockSpec(memory_space=pl.ANY),
         ],
-        out_specs=[pl.BlockSpec(memory_space=space) for space in (pl.ANY, pl.ANY, pltpu.VMEM, pl.ANY)],
+        out_specs=[pl.BlockSpec(memory_space=pl.ANY)] * 4,
         scratch_shapes=[
             pltpu.VMEM((SLOTS, stations, W), jnp.bfloat16),
             pltpu.VMEM((SLOTS, stations, W), jnp.float32),
             pltpu.VMEM((SLOTS, total), jnp.int32),
             pltpu.VMEM((stations, SLOTS * PH, W), jnp.bfloat16),
-            pltpu.VMEM((stations, SLOTS, LANES), jnp.float32),
+            pltpu.VMEM((SLOTS, LANES), jnp.float32),
             pltpu.VMEM((stations, following.shape[1]), jnp.bfloat16),
+            pltpu.VMEM((stations, W), jnp.bfloat16),
             pltpu.VMEM((stations // TURNS, SLOTS * PH, LANES), jnp.bfloat16),
         ]
-        + [pltpu.SemaphoreType.DMA] * 6,
+        + [pltpu.SemaphoreType.DMA] * 7,
         compiler_params=pltpu.CompilerParams(vmem_limit_bytes=VMEM),
         cost_estimate=pl.CostEstimate(flops=10_000_000, bytes_accessed=20_000_000, transcendentals=0),
         name="prepare",
     )(*(pltpu.with_memory_space_constraint(v, pltpu.HBM) for v in inputs))
 
 
-def correlate_kernel(chunk, moved, following, shifts, coef, edges, out, held, gains, edge, phases, inverse, windows, held_sems, gain_sem, edge_sem):
+def correlate_kernel(chunk, moved, following, shifts, coef, edges, out, held, gains, edge, tail, phases, inverse, windows, held_sems, gain_sem, edge_sem, tail_sem):
     owners, stations, block_len = moved.shape
     width = block_len // PH
     tiles = owners * block_len // (LANES * PH)
     per_tile = LANES // width
 
+    tail_copy = pltpu.make_async_copy(following, tail, tail_sem)
+    tail_copy.start()
     def held_copy(c):
         span = pl.ds(c * chunk, chunk)
         return pltpu.make_async_copy(shifts.at[span], held.at[span], held_sems.at[c])
 
-    held_copy(0).start()
     gain_copy = pltpu.make_async_copy(coef, gains, gain_sem)
     gain_copy.start()
     edge_copy = pltpu.make_async_copy(edges, edge, edge_sem)
     edge_copy.start()
+    for c in range(min(AHEAD, stations // chunk)):
+        held_copy(c).start()
 
     time = lax.broadcasted_iota(jnp.int32, (W, W), 0)
     place = lax.broadcasted_iota(jnp.int32, (W, W), 1)
@@ -243,7 +259,8 @@
     for j in range(tiles):
         pieces = [split(r) for r in rows[j * PIECES : (j + 1) * PIECES]]
         keep(phases, j, [v for h in range(PH // PIECES) for v in swap_groups([p[h] for p in pieces], TAPS)])
-    rows.append(following[...])
+    tail_copy.wait()
+    rows.append(tail[...])
     last = split(rows[-1])
     keep(
         phases,
@@ -310,8 +327,7 @@
                 corr = jnp.dot(held[s + e], window(s + e, turn + e, j), preferred_element_type=jnp.float32)
                 corr = (corr + ends[:, e * LANES : (e + 1) * LANES]).reshape(SLOTS, PH, LANES)
                 scale = inverse[j, s + e]
-                gain = [jnp.broadcast_to(gains[s + e, pl.ds(k, 1), :], (PH, LANES)) for k in range(SLOTS)]
-                total = tuple(total[k] + (corr[k] * scale) * gain[k] for k in range(SLOTS))
+                total = tuple(total[k] + (corr[k] * scale) * gains[k, s + e] for k in range(SLOTS))
             results.append(total)
         return tuple(results)
 
@@ -319,20 +335,22 @@
     gain_copy.wait()
     edge_copy.wait()
 
+    block = min(UNROLL, chunk)
+
     def part(c, totals):
         held_copy(c).wait()
 
-        @pl.when(c + 1 < stations // chunk)
+        @pl.when(c + AHEAD < stations // chunk)
         def _():
-            held_copy(c + 1).start()
+            held_copy(c + AHEAD).start()
 
         def some(i, totals):
-            for g in range(UNROLL // TURNS):
+            for g in range(block // TURNS):
                 for turn in range(0, TURNS, 2):
-                    totals = two_stations(c * (chunk // TURNS) + i * (UNROLL // TURNS) + g, turn, totals)
+                    totals = two_stations(c * (chunk // TURNS) + i * (block // TURNS) + g, turn, totals)
             return totals
 
-        return lax.fori_loop(0, chunk // UNROLL, some, totals)
+        return lax.fori_loop(0, chunk // block, some, totals)
 
     totals = lax.fori_loop(0, stations // chunk, part, totals)
 
@@ -354,7 +372,7 @@
         out_shape=jax.ShapeDtypeStruct((owners, NB, KB, LANES), jnp.float32),
         in_specs=[
             pl.BlockSpec(memory_space=pltpu.VMEM),
-            pl.BlockSpec(memory_space=pltpu.VMEM),
+            pl.BlockSpec(memory_space=pl.ANY),
             pl.BlockSpec(memory_space=pl.ANY),
             pl.BlockSpec(memory_space=pl.ANY),
             pl.BlockSpec(memory_space=pl.ANY),
@@ -362,23 +380,21 @@
         out_specs=pl.BlockSpec(memory_space=pltpu.VMEM),
         scratch_shapes=[
             pltpu.VMEM(shifts.shape, jnp.bfloat16),
-            pltpu.VMEM(coef.shape, jnp.float32),
+            pltpu.SMEM(coef.shape, jnp.float32),
             pltpu.VMEM(edges.shape, jnp.bfloat16),
+            pltpu.VMEM(following.shape, jnp.bfloat16),
             pltpu.VMEM((tiles + 1, stations, PH, LANES), jnp.float32),
             pltpu.VMEM((tiles, stations, PH, LANES), jnp.float32),
             pltpu.VMEM((len(MADE) + 1, tiles, 2, stations // 2, 2 * PH, LANES), jnp.bfloat16),
             pltpu.SemaphoreType.DMA((stations // chunk,)),
             pltpu.SemaphoreType.DMA,
             pltpu.SemaphoreType.DMA,
+            pltpu.SemaphoreType.DMA,
         ],
         compiler_params=pltpu.CompilerParams(vmem_limit_bytes=VMEM),
         cost_estimate=pl.CostEstimate(flops=1_200_000_000, bytes_accessed=10_000_000, transcendentals=0),
         name="correlate",
-    )(
-        moved,
-        pltpu.with_memory_space_constraint(following, pltpu.VMEM),
-        *(pltpu.with_memory_space_constraint(v, pltpu.HBM) for v in (shifts, coef, edges)),
-    )
+    )(moved, *(pltpu.with_memory_space_constraint(v, pltpu.HBM) for v in (following, shifts, coef, edges)))
 
 
 def shards(records, following, library, template_ids, channel_mask, station_group):

time: 36.7 us -> 34.6 us (0.943)
  Pallas kernels: 15.5 us -> 13.5 us
  waiting for transfers between devices: 1.56 us -> 2.23 us
  blocking collectives: 11.2 us -> 10.6 us
    pallas_call x1, Pallas kernels: 8.17 us -> 6.83 us  [correlate(): pl.pallas_call(functools.partial(correlate_kernel, chunk), out_shape=jax....]
    all_to_all x1, blocking collectives: 11.2 us -> 10.6 us  [shards(): lax.all_to_all(partial_sum.reshape(owners * NB, KB, block_len), ('tm', 's...]
    all_to_all x1, waiting for transfers between devices: 1.56 us -> 2.23 us  [shards(): lax.all_to_all(records.reshape(owners, stations, block_len), 'tm', split_...]
    pallas_call x1, Pallas kernels: 7.35 us -> 6.68 us  [prepare(): pl.pallas_call(prepare_kernel, out_shape=(pltpu.HBM((stations, SLOTS * PH...]
where the time goes in v6:
time: 34.6 us; the launch traced here: 34.2 us
  Pallas kernels  13.5 us (39%)
  blocking collectives  10.6 us (31%)
  starting transfers between devices  7.28 us (21%)
  waiting for transfers between devices  2.23 us (6%)
  other arithmetic  0.61 us (2%)
    all_to_all x1, blocking collectives, shards(): lax.all_to_all(partial_sum.reshape(owners * NB, KB, block_len), ('tm', 's...  10.6 us
    all_to_all x1, starting transfers between devices, shards(): lax.all_to_all(records.reshape(owners, stations, block_len), 'tm', split_...  7.28 us
    pallas_call x1, Pallas kernels, correlate(): pl.pallas_call(functools.partial(correlate_kernel, chunk), out_shape=jax....  6.83 us
    pallas_call x1, Pallas kernels, prepare(): pl.pallas_call(prepare_kernel, out_shape=(pltpu.HBM((stations, SLOTS * PH...  6.68 us
    all_to_all x1, waiting for transfers between devices, shards(): lax.all_to_all(records.reshape(owners, stations, block_len), 'tm', split_...  2.23 us
  transfers between devices with their start and end apart: 1, of which 1 were waited for; matrix products, arithmetic and copies ran while one was open for 0% of the time, Pallas kernels for 20%

profile of v6, /device:TPU:0, one launch (start us, length us, event | category | flops | bytes accessed | tf_op | source)
XLA Modules:
  0.0 34.2 jit_solution(17220653441616453760)
XLA Ops:
  0.0 7.3 %all-to-all-start = ((bf16[8,128,128]{2,1,0:T(8,128)(2,1)}), bf16[8,128,128]{2,1,0:T(8,128)(2,1)S(1)}, u32[]{:S(2)}, u32[]{:S(2)}) async-start(bf16[8,128,128]{2,1,0:T(8,128)(2,1)} %bitcast.5), calls=%async_computation | async-start | bytes 524288 | tf_op jit(solution)/shard_map/all_to_all | solution.py:404
  7.3 6.7 %prepare.1 = (bf16[128,128,256]{2,1,0:T(8,128)(2,1)}, f32[16,128]{1,0:T(8,128)}, bf16[128,256]{1,0:T(8,128)(2,1)}, bf16[8,128,128]{2,1,0:T(8,128)(2,1)}) custom-call(s32[2,8]{1,0:T(2,128)} %ids.1, bf16[32,128,256]{2,1,0:T(8,128)(2,1)} %library.1, s32[32,2048]{1,0:T(8,128)} %mask.1, s32[1,2048]{1,0:T(1,128)} %bitcast.6, bf16[1024,255]{1,0:T(8,128)(2,1)} %following.1), custom_call_target="tpu_custom_call" | custom-call | flops 10000000 | bytes 20000000 | tf_op jit(solution)/shard_map/prepare/pallas_call | solution.py:183
  14.0 2.2 %all-to-all-done.moved = bf16[8,128,128]{2,1,0:T(8,128)(2,1)S(1)} async-done(((bf16[8,128,128]{2,1,0:T(8,128)(2,1)}), bf16[8,128,128]{2,1,0:T(8,128)(2,1)S(1)}, u32[]{:S(2)}, u32[]{:S(2)}) %all-to-all-start) | async-done | bytes 262176 | tf_op jit(solution)/shard_map/all_to_all | solution.py:404
  16.2 6.8 %correlate.1 = f32[8,2,8,128]{3,2,1,0:T(8,128)S(1)} custom-call(bf16[8,128,128]{2,1,0:T(8,128)(2,1)S(1)} %all-to-all-done.moved, bf16[128,256]{1,0:T(8,128)(2,1)} %get-tuple-element.9.following, bf16[128,128,256]{2,1,0:T(8,128)(2,1)} %get-tuple-element.10.shifts, f32[16,128]{1,0:T(8,128)} %get-tuple-element.11.coef, bf16[8,128,128]{2,1,0:T(8,128)(2,1)} %get-tuple-element.12.edges), custom_call_target="tpu_custom_call" | custom-call | flops 1200000000 | bytes 10000000 | tf_op jit(solution)/shard_map/correlate/pallas_call | solution.py:370
  23.0 10.6 %all_to_all.10 = f32[16,8,128]{2,1,0:T(8,128)S(1)} all-to-all(f32[16,8,128]{2,1,0:T(8,128)S(1)} %bitcast.4), channel_id=1, replica_groups=mesh['days'=2,'tm'=8,'sta'=2] {'tm','sta'}, dimensions={0} | all-to-all | bytes 131072 | tf_op jit(solution)/shard_map/all_to_all | solution.py:407
  33.6 0.6 %reduce_sum.9 = f32[8,128]{1,0:T(8,128)} reduce(f32[16,8,128]{2,1,0:T(8,128)S(1)} %all_to_all.10, f32[]{:T(128)} %constant.0.clone.1), dimensions={0}, to_apply=%region_0.0 | reduce | flops 15360 | bytes 69636 | tf_op jit(solution)/shard_map/reduce_sum | solution.py:410
Async XLA Ops:
  0.0 16.2 %all-to-all-start = ((bf16[8,128,128]{2,1,0:T(8,128)(2,1)}), bf16[8,128,128]{2,1,0:T(8,128)(2,1)S(1)}, u32[]{:S(2)}, u32[]{:S(2)}) async-start(bf16[8,128,128]{2,1,0:T(8,128)(2,1)} %bitcast.5), calls=%async_computation | async-start | bytes 524288 | tf_op jit(solution)/shard_map/all_to_all | solution.py:404

commit v7 on v6

--- a/solution.py
+++ b/solution.py
@@ -1,5 +1,4 @@
 import functools
-import math
 
 import jax
 import jax.numpy as jnp
@@ -18,9 +17,8 @@
 TAPS = W // PH
 PIECES = LANES // TAPS
 VMEM = 24 << 20
-CHUNK = 64
-AHEAD = 1
-UNROLL = 64
+PARTS = (48, 80)
+START = (0, 1)
 TURNS = LANES // PH
 MADE = (8, 4)
 
@@ -213,7 +211,7 @@
     )(*(pltpu.with_memory_space_constraint(v, pltpu.HBM) for v in inputs))
 
 
-def correlate_kernel(chunk, moved, following, shifts, coef, edges, out, held, gains, edge, tail, phases, inverse, windows, held_sems, gain_sem, edge_sem, tail_sem):
+def correlate_kernel(moved, following, shifts, coef, edges, out, held, gains, edge, tail, phases, inverse, windows, held_sems, gain_sem, edge_sem, tail_sem):
     owners, stations, block_len = moved.shape
     width = block_len // PH
     tiles = owners * block_len // (LANES * PH)
@@ -221,16 +219,25 @@
 
     tail_copy = pltpu.make_async_copy(following, tail, tail_sem)
     tail_copy.start()
-    def held_copy(c):
-        span = pl.ds(c * chunk, chunk)
-        return pltpu.make_async_copy(shifts.at[span], held.at[span], held_sems.at[c])
+    bounds = [0]
+    for size in PARTS:
+        bounds.append(min(stations, bounds[-1] + size))
+    bounds[-1] = stations
+
+    def held_copies(stage):
+        for n, when in enumerate(START):
+            if when == stage and bounds[n] < bounds[n + 1]:
+                held_copy(n).start()
+
+    def held_copy(n):
+        span = pl.ds(bounds[n], bounds[n + 1] - bounds[n])
+        return pltpu.make_async_copy(shifts.at[span], held.at[span], held_sems.at[n])
 
     gain_copy = pltpu.make_async_copy(coef, gains, gain_sem)
     gain_copy.start()
     edge_copy = pltpu.make_async_copy(edges, edge, edge_sem)
     edge_copy.start()
-    for c in range(min(AHEAD, stations // chunk)):
-        held_copy(c).start()
+    held_copies(0)
 
     time = lax.broadcasted_iota(jnp.int32, (W, W), 0)
     place = lax.broadcasted_iota(jnp.int32, (W, W), 1)
@@ -271,6 +278,8 @@
         ],
     )
 
+    held_copies(1)
+
     ahead = time - place % LANES - place // LANES
     for parity in range(2):
         for n in range(len(MADE) + 1):
@@ -335,24 +344,14 @@
     gain_copy.wait()
     edge_copy.wait()
 
-    block = min(UNROLL, chunk)
-
-    def part(c, totals):
-        held_copy(c).wait()
-
-        @pl.when(c + AHEAD < stations // chunk)
-        def _():
-            held_copy(c + AHEAD).start()
-
-        def some(i, totals):
-            for g in range(block // TURNS):
-                for turn in range(0, TURNS, 2):
-                    totals = two_stations(c * (chunk // TURNS) + i * (block // TURNS) + g, turn, totals)
-            return totals
-
-        return lax.fori_loop(0, chunk // block, some, totals)
-
-    totals = lax.fori_loop(0, stations // chunk, part, totals)
+    for n in range(len(PARTS)):
+        if bounds[n] < bounds[n + 1]:
+            if n == 0:
+                held_copies(2)
+            held_copy(n).wait()
+            held_copies(3 + n)
+            for s in range(bounds[n], bounds[n + 1], 2):
+                totals = two_stations(s // TURNS, s % TURNS, totals)
 
     lane = lane_ids((KB, LANES))
     source = lane % PH * width + lane // PH
@@ -366,9 +365,8 @@
 def correlate(moved, following, shifts, coef, edges):
     owners, stations, block_len = moved.shape
     tiles = owners * block_len // (LANES * PH)
-    chunk = math.gcd(stations, CHUNK)
     return pl.pallas_call(
-        functools.partial(correlate_kernel, chunk),
+        correlate_kernel,
         out_shape=jax.ShapeDtypeStruct((owners, NB, KB, LANES), jnp.float32),
         in_specs=[
             pl.BlockSpec(memory_space=pltpu.VMEM),
@@ -386,7 +384,7 @@
             pltpu.VMEM((tiles + 1, stations, PH, LANES), jnp.float32),
             pltpu.VMEM((tiles, stations, PH, LANES), jnp.float32),
             pltpu.VMEM((len(MADE) + 1, tiles, 2, stations // 2, 2 * PH, LANES), jnp.bfloat16),
-            pltpu.SemaphoreType.DMA((stations // chunk,)),
+            pltpu.SemaphoreType.DMA((len(PARTS),)),
             pltpu.SemaphoreType.DMA,
             pltpu.SemaphoreType.DMA,
             pltpu.SemaphoreType.DMA,

time: 34.6 us -> 34.2 us (0.988)
  Pallas kernels: 13.5 us -> 13.1 us
    pallas_call x1, Pallas kernels: 6.83 us -> 6.45 us  [correlate(): pl.pallas_call(correlate_kernel, out_shape=jax.ShapeDtypeStruct((owners,...]
where the time goes in v7:
time: 34.2 us; the launch traced here: 33.8 us
  Pallas kernels  13.1 us (38%)
  blocking collectives  10.6 us (31%)
  starting transfers between devices  7.28 us (21%)
  waiting for transfers between devices  2.23 us (7%)
  other arithmetic  0.61 us (2%)
    all_to_all x1, blocking collectives, shards(): lax.all_to_all(partial_sum.reshape(owners * NB, KB, block_len), ('tm', 's...  10.6 us
    all_to_all x1, starting transfers between devices, shards(): lax.all_to_all(records.reshape(owners, stations, block_len), 'tm', split_...  7.28 us
    pallas_call x1, Pallas kernels, prepare(): pl.pallas_call(prepare_kernel, out_shape=(pltpu.HBM((stations, SLOTS * PH...  6.68 us
    pallas_call x1, Pallas kernels, correlate(): pl.pallas_call(correlate_kernel, out_shape=jax.ShapeDtypeStruct((owners,...  6.45 us
    all_to_all x1, waiting for transfers between devices, shards(): lax.all_to_all(records.reshape(owners, stations, block_len), 'tm', split_...  2.23 us
  transfers between devices with their start and end apart: 1, of which 1 were waited for; matrix products, arithmetic and copies ran while one was open for 0% of the time, Pallas kernels for 20%

profile of v7, /device:TPU:0, one launch (start us, length us, event | category | flops | bytes accessed | tf_op | source)
XLA Modules:
  0.0 33.8 jit_solution(13106039828580019691)
XLA Ops:
  0.0 7.3 %all-to-all-start = ((bf16[8,128,128]{2,1,0:T(8,128)(2,1)}), bf16[8,128,128]{2,1,0:T(8,128)(2,1)S(1)}, u32[]{:S(2)}, u32[]{:S(2)}) async-start(bf16[8,128,128]{2,1,0:T(8,128)(2,1)} %bitcast.5), calls=%async_computation | async-start | bytes 524288 | tf_op jit(solution)/shard_map/all_to_all | solution.py:402
  7.3 6.7 %prepare.1 = (bf16[128,128,256]{2,1,0:T(8,128)(2,1)}, f32[16,128]{1,0:T(8,128)}, bf16[128,256]{1,0:T(8,128)(2,1)}, bf16[8,128,128]{2,1,0:T(8,128)(2,1)}) custom-call(s32[2,8]{1,0:T(2,128)} %ids.1, bf16[32,128,256]{2,1,0:T(8,128)(2,1)} %library.1, s32[32,2048]{1,0:T(8,128)} %mask.1, s32[1,2048]{1,0:T(1,128)} %bitcast.6, bf16[1024,255]{1,0:T(8,128)(2,1)} %following.1), custom_call_target="tpu_custom_call" | custom-call | flops 10000000 | bytes 20000000 | tf_op jit(solution)/shard_map/prepare/pallas_call | solution.py:181
  14.0 2.2 %all-to-all-done.moved = bf16[8,128,128]{2,1,0:T(8,128)(2,1)S(1)} async-done(((bf16[8,128,128]{2,1,0:T(8,128)(2,1)}), bf16[8,128,128]{2,1,0:T(8,128)(2,1)S(1)}, u32[]{:S(2)}, u32[]{:S(2)}) %all-to-all-start) | async-done | bytes 262176 | tf_op jit(solution)/shard_map/all_to_all | solution.py:402
  16.2 6.4 %correlate.1 = f32[8,2,8,128]{3,2,1,0:T(8,128)S(1)} custom-call(bf16[8,128,128]{2,1,0:T(8,128)(2,1)S(1)} %all-to-all-done.moved, bf16[128,256]{1,0:T(8,128)(2,1)} %get-tuple-element.9.following, bf16[128,128,256]{2,1,0:T(8,128)(2,1)} %get-tuple-element.10.shifts, f32[16,128]{1,0:T(8,128)} %get-tuple-element.11.coef, bf16[8,128,128]{2,1,0:T(8,128)(2,1)} %get-tuple-element.12.edges), custom_call_target="tpu_custom_call" | custom-call | flops 1200000000 | bytes 10000000 | tf_op jit(solution)/shard_map/correlate/pallas_call | solution.py:368
  22.7 10.6 %all_to_all.10 = f32[16,8,128]{2,1,0:T(8,128)S(1)} all-to-all(f32[16,8,128]{2,1,0:T(8,128)S(1)} %bitcast.4), channel_id=1, replica_groups=mesh['days'=2,'tm'=8,'sta'=2] {'tm','sta'}, dimensions={0} | all-to-all | bytes 131072 | tf_op jit(solution)/shard_map/all_to_all | solution.py:405
  33.2 0.6 %reduce_sum.9 = f32[8,128]{1,0:T(8,128)} reduce(f32[16,8,128]{2,1,0:T(8,128)S(1)} %all_to_all.10, f32[]{:T(128)} %constant.0.clone.1), dimensions={0}, to_apply=%region_0.0 | reduce | flops 15360 | bytes 69636 | tf_op jit(solution)/shard_map/reduce_sum | solution.py:408
Async XLA Ops:
  0.0 16.2 %all-to-all-start = ((bf16[8,128,128]{2,1,0:T(8,128)(2,1)}), bf16[8,128,128]{2,1,0:T(8,128)(2,1)S(1)}, u32[]{:S(2)}, u32[]{:S(2)}) async-start(bf16[8,128,128]{2,1,0:T(8,128)(2,1)} %bitcast.5), calls=%async_computation | async-start | bytes 524288 | tf_op jit(solution)/shard_map/all_to_all | solution.py:402

commit v8 on v7

--- a/solution.py
+++ b/solution.py
@@ -236,8 +236,8 @@
     gain_copy = pltpu.make_async_copy(coef, gains, gain_sem)
     gain_copy.start()
     edge_copy = pltpu.make_async_copy(edges, edge, edge_sem)
+    held_copies(0)
     edge_copy.start()
-    held_copies(0)
 
     time = lax.broadcasted_iota(jnp.int32, (W, W), 0)
     place = lax.broadcasted_iota(jnp.int32, (W, W), 1)
@@ -266,6 +266,22 @@
     for j in range(tiles):
         pieces = [split(r) for r in rows[j * PIECES : (j + 1) * PIECES]]
         keep(phases, j, [v for h in range(PH // PIECES) for v in swap_groups([p[h] for p in pieces], TAPS)])
+
+    squared = [squares(r) for r in rows]
+    for j in range(tiles):
+        pieces = []
+        for q in range(j * PIECES, (j + 1) * PIECES):
+            terms = [(part, here) for part in squared[q]]
+            if q + 1 < len(rows):
+                terms += [(part, beyond) for part in squared[q + 1]]
+            energy = sum(jnp.dot(part, matrix, preferred_element_type=jnp.float32) for part, matrix in terms)
+            pieces.append([energy[:, h * LANES : (h + 1) * LANES] for h in range(W // LANES)])
+        values = [v for h in range(PH // PIECES) for v in swap_groups([p[h] for p in pieces], TAPS)]
+        if j < tiles - 1:
+            values = [lax.rsqrt(v / W + epsilon) for v in values]
+        keep(inverse, j, values)
+
+    held_copies(1)
     tail_copy.wait()
     rows.append(tail[...])
     last = split(rows[-1])
@@ -277,8 +293,6 @@
             for p in range(PH)
         ],
     )
-
-    held_copies(1)
 
     ahead = time - place % LANES - place // LANES
     for parity in range(2):
@@ -295,18 +309,16 @@
                 value = [value[:, h * LANES : (h + 1) * LANES].reshape(stations // 2, PH, LANES) for h in range(2)]
                 windows[n, j, parity] = jnp.concatenate(value, axis=1).astype(jnp.bfloat16)
 
-    squared = [squares(r) for r in rows]
-    for j in range(tiles):
-        pieces = []
-        for q in range(j * PIECES, (j + 1) * PIECES):
-            energy = sum(
-                jnp.dot(part, matrix, preferred_element_type=jnp.float32)
-                for parts, matrix in ((squared[q], here), (squared[q + 1], beyond))
-                for part in parts
-            )
-            energy = lax.rsqrt(energy / W + epsilon)
-            pieces.append([energy[:, h * LANES : (h + 1) * LANES] for h in range(W // LANES)])
-        keep(inverse, j, [v for h in range(PH // PIECES) for v in swap_groups([p[h] for p in pieces], TAPS)])
+    extra = sum(jnp.dot(part, beyond, preferred_element_type=jnp.float32) for part in squares(rows[-1]))
+    lane = lane_ids((stations, LANES))
+    parts = []
+    for p in range(PH):
+        piece = extra[:, p // PIECES * LANES : (p // PIECES + 1) * LANES]
+        if p % PIECES != PIECES - 1:
+            piece = pltpu.roll(piece, TAPS * (PIECES - 1 - p % PIECES), 1)
+        parts.append(jnp.where(lane >= LANES - TAPS, piece, 0.0))
+    parts = jnp.swapaxes(jnp.stack(parts), 0, 1)
+    inverse[tiles - 1] = lax.rsqrt((inverse[tiles - 1] + parts) / W + epsilon)
 
     nothing = jnp.zeros((2 * PH, LANES), jnp.bfloat16)
 

time: 34.2 us -> 34.2 us (level)
  no operation moved by 1% of the time
where the time goes in v8:
time: 34.2 us; the launch traced here: 33.9 us
  Pallas kernels  13.2 us (39%)
  blocking collectives  10.6 us (31%)
  starting transfers between devices  7.28 us (21%)
  waiting for transfers between devices  2.23 us (7%)
  other arithmetic  0.61 us (2%)
    all_to_all x1, blocking collectives, shards(): lax.all_to_all(partial_sum.reshape(owners * NB, KB, block_len), ('tm', 's...  10.6 us
    all_to_all x1, starting transfers between devices, shards(): lax.all_to_all(records.reshape(owners, stations, block_len), 'tm', split_...  7.28 us
    pallas_call x1, Pallas kernels, prepare(): pl.pallas_call(prepare_kernel, out_shape=(pltpu.HBM((stations, SLOTS * PH...  6.68 us
    pallas_call x1, Pallas kernels, correlate(): pl.pallas_call(correlate_kernel, out_shape=jax.ShapeDtypeStruct((owners,...  6.47 us
    all_to_all x1, waiting for transfers between devices, shards(): lax.all_to_all(records.reshape(owners, stations, block_len), 'tm', split_...  2.23 us
  transfers between devices with their start and end apart: 1, of which 1 were waited for; matrix products, arithmetic and copies ran while one was open for 0% of the time, Pallas kernels for 20%

profile of v8, /device:TPU:0, one launch (start us, length us, event | category | flops | bytes accessed | tf_op | source)
XLA Modules:
  0.0 33.9 jit_solution(11063317770495644980)
XLA Ops:
  0.0 7.3 %all-to-all-start = ((bf16[8,128,128]{2,1,0:T(8,128)(2,1)}), bf16[8,128,128]{2,1,0:T(8,128)(2,1)S(1)}, u32[]{:S(2)}, u32[]{:S(2)}) async-start(bf16[8,128,128]{2,1,0:T(8,128)(2,1)} %bitcast.5), calls=%async_computation | async-start | bytes 524288 | tf_op jit(solution)/shard_map/all_to_all | solution.py:414
  7.3 6.7 %prepare.1 = (bf16[128,128,256]{2,1,0:T(8,128)(2,1)}, f32[16,128]{1,0:T(8,128)}, bf16[128,256]{1,0:T(8,128)(2,1)}, bf16[8,128,128]{2,1,0:T(8,128)(2,1)}) custom-call(s32[2,8]{1,0:T(2,128)} %ids.1, bf16[32,128,256]{2,1,0:T(8,128)(2,1)} %library.1, s32[32,2048]{1,0:T(8,128)} %mask.1, s32[1,2048]{1,0:T(1,128)} %bitcast.6, bf16[1024,255]{1,0:T(8,128)(2,1)} %following.1), custom_call_target="tpu_custom_call" | custom-call | flops 10000000 | bytes 20000000 | tf_op jit(solution)/shard_map/prepare/pallas_call | solution.py:181
  14.0 2.2 %all-to-all-done.moved = bf16[8,128,128]{2,1,0:T(8,128)(2,1)S(1)} async-done(((bf16[8,128,128]{2,1,0:T(8,128)(2,1)}), bf16[8,128,128]{2,1,0:T(8,128)(2,1)S(1)}, u32[]{:S(2)}, u32[]{:S(2)}) %all-to-all-start) | async-done | bytes 262176 | tf_op jit(solution)/shard_map/all_to_all | solution.py:414
  16.2 6.5 %correlate.1 = f32[8,2,8,128]{3,2,1,0:T(8,128)S(1)} custom-call(bf16[8,128,128]{2,1,0:T(8,128)(2,1)S(1)} %all-to-all-done.moved, bf16[128,256]{1,0:T(8,128)(2,1)} %get-tuple-element.9.following, bf16[128,128,256]{2,1,0:T(8,128)(2,1)} %get-tuple-element.10.shifts, f32[16,128]{1,0:T(8,128)} %get-tuple-element.11.coef, bf16[8,128,128]{2,1,0:T(8,128)(2,1)} %get-tuple-element.12.edges), custom_call_target="tpu_custom_call" | custom-call | flops 1200000000 | bytes 10000000 | tf_op jit(solution)/shard_map/correlate/pallas_call | solution.py:380
  22.7 10.6 %all_to_all.10 = f32[16,8,128]{2,1,0:T(8,128)S(1)} all-to-all(f32[16,8,128]{2,1,0:T(8,128)S(1)} %bitcast.4), channel_id=1, replica_groups=mesh['days'=2,'tm'=8,'sta'=2] {'tm','sta'}, dimensions={0} | all-to-all | bytes 131072 | tf_op jit(solution)/shard_map/all_to_all | solution.py:417
  33.3 0.6 %reduce_sum.9 = f32[8,128]{1,0:T(8,128)} reduce(f32[16,8,128]{2,1,0:T(8,128)S(1)} %all_to_all.10, f32[]{:T(128)} %constant.0.clone.1), dimensions={0}, to_apply=%region_0.0 | reduce | flops 15360 | bytes 69636 | tf_op jit(solution)/shard_map/reduce_sum | solution.py:420
Async XLA Ops:
  0.0 16.2 %all-to-all-start = ((bf16[8,128,128]{2,1,0:T(8,128)(2,1)}), bf16[8,128,128]{2,1,0:T(8,128)(2,1)S(1)}, u32[]{:S(2)}, u32[]{:S(2)}) async-start(bf16[8,128,128]{2,1,0:T(8,128)(2,1)} %bitcast.5), calls=%async_computation | async-start | bytes 524288 | tf_op jit(solution)/shard_map/all_to_all | solution.py:414

commit v9 on v7

--- a/solution.py
+++ b/solution.py
@@ -17,7 +17,7 @@
 TAPS = W // PH
 PIECES = LANES // TAPS
 VMEM = 24 << 20
-PARTS = (48, 80)
+PARTS = (56, 72)
 START = (0, 1)
 TURNS = LANES // PH
 MADE = (8, 4)

time: 34.2 us -> 34.2 us (level)
  no operation moved by 1% of the time
where the time goes in v9:
time: 34.2 us; the launch traced here: 33.8 us
  Pallas kernels  13.1 us (38%)
  blocking collectives  10.6 us (31%)
  starting transfers between devices  7.28 us (21%)
  waiting for transfers between devices  2.23 us (7%)
  other arithmetic  0.61 us (2%)
    all_to_all x1, blocking collectives, shards(): lax.all_to_all(partial_sum.reshape(owners * NB, KB, block_len), ('tm', 's...  10.6 us
    all_to_all x1, starting transfers between devices, shards(): lax.all_to_all(records.reshape(owners, stations, block_len), 'tm', split_...  7.28 us
    pallas_call x1, Pallas kernels, prepare(): pl.pallas_call(prepare_kernel, out_shape=(pltpu.HBM((stations, SLOTS * PH...  6.68 us
    pallas_call x1, Pallas kernels, correlate(): pl.pallas_call(correlate_kernel, out_shape=jax.ShapeDtypeStruct((owners,...  6.41 us
    all_to_all x1, waiting for transfers between devices, shards(): lax.all_to_all(records.reshape(owners, stations, block_len), 'tm', split_...  2.23 us
  transfers between devices with their start and end apart: 1, of which 1 were waited for; matrix products, arithmetic and copies ran while one was open for 0% of the time, Pallas kernels for 20%

profile of v9, /device:TPU:0, one launch (start us, length us, event | category | flops | bytes accessed | tf_op | source)
XLA Modules:
  0.0 33.8 jit_solution(10805682835159060832)
XLA Ops:
  0.0 7.3 %all-to-all-start = ((bf16[8,128,128]{2,1,0:T(8,128)(2,1)}), bf16[8,128,128]{2,1,0:T(8,128)(2,1)S(1)}, u32[]{:S(2)}, u32[]{:S(2)}) async-start(bf16[8,128,128]{2,1,0:T(8,128)(2,1)} %bitcast.5), calls=%async_computation | async-start | bytes 524288 | tf_op jit(solution)/shard_map/all_to_all | solution.py:402
  7.3 6.7 %prepare.1 = (bf16[128,128,256]{2,1,0:T(8,128)(2,1)}, f32[16,128]{1,0:T(8,128)}, bf16[128,256]{1,0:T(8,128)(2,1)}, bf16[8,128,128]{2,1,0:T(8,128)(2,1)}) custom-call(s32[2,8]{1,0:T(2,128)} %ids.1, bf16[32,128,256]{2,1,0:T(8,128)(2,1)} %library.1, s32[32,2048]{1,0:T(8,128)} %mask.1, s32[1,2048]{1,0:T(1,128)} %bitcast.6, bf16[1024,255]{1,0:T(8,128)(2,1)} %following.1), custom_call_target="tpu_custom_call" | custom-call | flops 10000000 | bytes 20000000 | tf_op jit(solution)/shard_map/prepare/pallas_call | solution.py:181
  14.0 2.2 %all-to-all-done.moved = bf16[8,128,128]{2,1,0:T(8,128)(2,1)S(1)} async-done(((bf16[8,128,128]{2,1,0:T(8,128)(2,1)}), bf16[8,128,128]{2,1,0:T(8,128)(2,1)S(1)}, u32[]{:S(2)}, u32[]{:S(2)}) %all-to-all-start) | async-done | bytes 262176 | tf_op jit(solution)/shard_map/all_to_all | solution.py:402
  16.2 6.4 %correlate.1 = f32[8,2,8,128]{3,2,1,0:T(8,128)S(1)} custom-call(bf16[8,128,128]{2,1,0:T(8,128)(2,1)S(1)} %all-to-all-done.moved, bf16[128,256]{1,0:T(8,128)(2,1)} %get-tuple-element.9.following, bf16[128,128,256]{2,1,0:T(8,128)(2,1)} %get-tuple-element.10.shifts, f32[16,128]{1,0:T(8,128)} %get-tuple-element.11.coef, bf16[8,128,128]{2,1,0:T(8,128)(2,1)} %get-tuple-element.12.edges), custom_call_target="tpu_custom_call" | custom-call | flops 1200000000 | bytes 10000000 | tf_op jit(solution)/shard_map/correlate/pallas_call | solution.py:368
  22.6 10.6 %all_to_all.10 = f32[16,8,128]{2,1,0:T(8,128)S(1)} all-to-all(f32[16,8,128]{2,1,0:T(8,128)S(1)} %bitcast.4), channel_id=1, replica_groups=mesh['days'=2,'tm'=8,'sta'=2] {'tm','sta'}, dimensions={0} | all-to-all | bytes 131072 | tf_op jit(solution)/shard_map/all_to_all | solution.py:405
  33.2 0.6 %reduce_sum.9 = f32[8,128]{1,0:T(8,128)} reduce(f32[16,8,128]{2,1,0:T(8,128)S(1)} %all_to_all.10, f32[]{:T(128)} %constant.0.clone.1), dimensions={0}, to_apply=%region_0.0 | reduce | flops 15360 | bytes 69636 | tf_op jit(solution)/shard_map/reduce_sum | solution.py:408
Async XLA Ops:
  0.0 16.2 %all-to-all-start = ((bf16[8,128,128]{2,1,0:T(8,128)(2,1)}), bf16[8,128,128]{2,1,0:T(8,128)(2,1)S(1)}, u32[]{:S(2)}, u32[]{:S(2)}) async-start(bf16[8,128,128]{2,1,0:T(8,128)(2,1)} %bitcast.5), calls=%async_computation | async-start | bytes 524288 | tf_op jit(solution)/shard_map/all_to_all | solution.py:402
